TPU v7x, 32 devices: a whole 2x2x4 slice. The times are simulated.
32 devices in a mesh: seq: 4 (over y, core), exp: 8 (over z, x).
Axes of the slice: x: 2, y: 2, z: 4, core: 2. Of those that a mesh axis runs over, the one named last changes fastest.
Arguments:
- tokens: bfloat16 [8, 2048, 1280], P('exp', 'seq'), may hold values from -64 to 64
- router: bfloat16 [1280, 16], replicated, may hold values from -2 to 2
- w_in: bfloat16 [8, 1280, 5120], P('exp', None, 'seq'), may hold values from -0.15625 to 0.15625
- w_out: bfloat16 [8, 5120, 1280], P('exp', 'seq'), may hold values from -0.078125 to 0.078125
- grad_out: bfloat16 [8, 2048, 1280], P('exp', 'seq'), may hold values from -6 to 6
Outputs:
- mixed: bfloat16 [8, 2048, 1280], P('exp', 'seq')
- d_tokens: bfloat16 [8, 2048, 1280], P('exp', 'seq')
- d_router: float32 [1280, 16], P(('seq', 'exp'))
- d_w_in: bfloat16 [8, 1280, 5120], P('exp', None, 'seq')
- d_w_out: bfloat16 [8, 5120, 1280], P('exp', 'seq')
All inputs are finite; a program needn't handle non-finite values.
Results may differ from a plain program's by a relative error of at most 0.034.
Values may be sent and summed in bfloat16 or wider, within the bound.
No kernel may reach another device: no remote copies, remote signals or barrier semaphores. Data moves between devices by JAX's collectives and lax.ppermute only.
A program may use at most 64 MiB of HBM per device.

v0:
```python
import math

import jax
import jax.numpy as jnp
from jax import lax
from jax.sharding import PartitionSpec as P


def gelu_grad(values):
    return 0.5 * (1.0 + lax.erf(values * (1.0 / math.sqrt(2.0)))) + values * jnp.exp(
        -0.5 * values * values
    ) / math.sqrt(2.0 * math.pi)


def to_experts(partial_value):
    summed = lax.psum(partial_value, "seq").astype(jnp.bfloat16)
    return lax.all_to_all(summed, "exp", split_axis=1, concat_axis=0, tiled=True)


def from_experts(partial_value):
    summed = lax.psum(partial_value.astype(jnp.bfloat16), "seq")
    return lax.all_to_all(summed, "exp", split_axis=0, concat_axis=1, tiled=True)


def shards(tokens, router, w_in, w_out, grad_out):
    feats = tokens[0]
    cotangent = grad_out[0]
    width = feats.shape[1]
    logits = lax.dot_general(
        router, feats, (((0,), (1,)), ((), ())), preferred_element_type=jnp.float32
    )
    col_top = lax.pmax(jnp.max(logits, axis=1), "seq")
    col_exp = jnp.exp(logits - col_top[:, None])
    col_total = lax.psum(jnp.sum(col_exp, axis=1), "seq")
    dispatch = col_exp / col_total[:, None]
    dispatch_b = dispatch.astype(jnp.bfloat16)
    partial_in = jnp.dot(dispatch_b, feats, preferred_element_type=jnp.float32)
    row_top = jnp.max(logits, axis=0, keepdims=True)
    row_exp = jnp.exp(logits - row_top)
    combine = row_exp / jnp.sum(row_exp, axis=0, keepdims=True)
    combine_b = combine.astype(jnp.bfloat16)
    rows_in = to_experts(partial_in[None])
    rows = rows_in.reshape(-1, width)
    hidden = jnp.dot(rows, w_in[0], preferred_element_type=jnp.float32)
    activated = jax.nn.gelu(hidden, approximate=False).astype(jnp.bfloat16)
    out_part = jnp.dot(activated, w_out[0], preferred_element_type=jnp.float32)
    slot_output = from_experts(out_part.reshape(rows_in.shape))[0]
    mixed = lax.dot_general(
        combine_b, slot_output, (((0,), (0,)), ((), ())), preferred_element_type=jnp.float32
    ).astype(jnp.bfloat16)
    d_combine = lax.dot_general(
        slot_output, cotangent, (((1,), (1,)), ((), ())), preferred_element_type=jnp.float32
    )
    d_logit_c = combine * (d_combine - jnp.sum(combine * d_combine, axis=0, keepdims=True))
    d_out_part = jnp.dot(combine_b, cotangent, preferred_element_type=jnp.float32)
    d_rows = to_experts(d_out_part[None]).reshape(-1, width)
    d_activated = lax.dot_general(
        d_rows, w_out[0], (((1,), (1,)), ((), ())), preferred_element_type=jnp.float32
    )
    d_hidden = (d_activated * gelu_grad(hidden)).astype(jnp.bfloat16)
    d_w_out = lax.dot_general(
        activated, d_rows, (((0,), (0,)), ((), ())), preferred_element_type=jnp.float32
    )
    d_w_in = lax.dot_general(
        rows, d_hidden, (((0,), (0,)), ((), ())), preferred_element_type=jnp.float32
    )
    d_in_part = lax.dot_general(
        d_hidden, w_in[0], (((1,), (1,)), ((), ())), preferred_element_type=jnp.float32
    )
    slot_input_gradient = from_experts(d_in_part.reshape(rows_in.shape))[0]
    d_dispatch = lax.dot_general(
        slot_input_gradient, feats, (((1,), (1,)), ((), ())), preferred_element_type=jnp.float32
    )
    column_sum = lax.psum(jnp.sum(dispatch * d_dispatch, axis=1), "seq")
    d_logit_d = dispatch * (d_dispatch - column_sum[:, None])
    d_logit_b = (d_logit_c + d_logit_d).astype(jnp.bfloat16)
    d_feats = lax.dot_general(
        dispatch_b,
        slot_input_gradient,
        (((0,), (0,)), ((), ())),
        preferred_element_type=jnp.float32,
    )
    d_feats = d_feats + lax.dot_general(
        d_logit_b, router, (((0,), (1,)), ((), ())), preferred_element_type=jnp.float32
    )
    d_router = lax.psum_scatter(
        lax.dot_general(
            feats, d_logit_b, (((0,), (1,)), ((), ())), preferred_element_type=jnp.float32
        ),
        ("seq", "exp"),
        scatter_dimension=0,
        tiled=True,
    )
    return (
        mixed[None],
        d_feats.astype(jnp.bfloat16)[None],
        d_router,
        d_w_in.astype(jnp.bfloat16)[None],
        d_w_out.astype(jnp.bfloat16)[None],
    )


def solution(mesh):
    in_specs = (
        P("exp", "seq", None),
        P(),
        P("exp", None, "seq"),
        P("exp", "seq", None),
        P("exp", "seq", None),
    )
    out_specs = (
        P("exp", "seq", None),
        P("exp", "seq", None),
        P(("seq", "exp"), None),
        P("exp", None, "seq"),
        P("exp", "seq", None),
    )
    return jax.shard_map(shards, mesh=mesh, in_specs=in_specs, out_specs=out_specs, check_vma=False)
```

profile of v0, /device:TPU:0, one launch (start us, length us, event | category | flops | bytes accessed | tf_op | source)
XLA Modules:
  0.0 260.5 jit_solution(8110577711762016141)
XLA Ops:
  7.2 0.0 copy-start
  7.2 2.1 fusion.71
  9.2 0.0 copy-start.3
  9.2 8.4 %pmax.7 = f32[16]{0:T(128)S(1)} all-reduce(f32[16]{0:T(128)S(1)} %get-tuple-element.10), channel_id=1, replica_groups=mesh['seq'=4,'exp'=8] {'seq'}, use_global_device_ids=true, to_apply=%region_3.0 | all-reduce | flops 16 | bytes 128 | tf_op jit(solution)/shard_map/pmax | solution.py:32
  17.6 0.0 copy-start.8
  17.6 0.2 fusion.55
  17.8 0.0 copy-start.5
  17.8 0.6 copy-done.5
  18.4 1.6 convolution_bitcast_fusion.1
  20.0 0.0 copy-done.3
  20.0 5.7 %psum.42 = f32[16]{0:T(128)S(1)} all-reduce(f32[16]{0:T(128)S(1)} %get-tuple-element.8), channel_id=1, replica_groups=mesh['seq'=4,'exp'=8] {'seq'}, use_global_device_ids=true, to_apply=%region_5.0 | all-reduce | flops 16 | bytes 128 | tf_op jit(solution)/shard_map/psum | solution.py:34
  25.7 0.0 copy-done.8
  25.7 0.0 copy-start.10
  25.7 0.6 copy-done.10
  26.3 1.6 convolution_bitcast_fusion.2
  28.0 12.1 %all-reduce.10 = (bf16[1,16,1280]{2,1,0:T(8,128)(2,1)S(1)}, bf16[1,16,1280]{2,1,0:T(8,128)(2,1)S(1)}) all-reduce(f32[1,16,1280]{2,1,0:T(8,128)S(1)} %convolution_bitcast_fusion.2, f32[1,16,1280]{2,1,0:T(8,128)S(1)} %convolution_bitcast_fusion.1), channel_id=1, replica_groups=mesh['seq'=4,'exp'=8] {'seq'}, use_global_device_ids=true, to_apply=%region_6.0 | all-reduce | flops 40960 | bytes 245760 | tf_op jit(solution)/shard_map/psum | solution.py:16
  40.0 0.1 copy.57
  40.1 0.5 broadcast.25
  40.6 0.9 reduce
  41.5 0.6 reshape.48
  42.1 6.0 %all-to-all-start = ((bf16[8,2,1280]{2,1,0:T(2,128)(2,1)}), bf16[8,2,1280]{2,1,0:T(2,128)(2,1)S(1)}, u32[]{:S(2)}, u32[]{:S(2)}) async-start(bf16[8,2,1280]{2,1,0:T(2,128)(2,1)} %reshape.48), calls=%async_computation | async-start | bytes 81920 | tf_op jit(solution)/shard_map/all_to_all | solution.py:17
  48.1 0.1 copy.56
  48.2 0.9 reduce.1
  49.0 0.6 reshape.50
  49.7 5.2 %all-to-all-done = bf16[8,2,1280]{2,1,0:T(2,128)(2,1)S(1)} async-done(((bf16[8,2,1280]{2,1,0:T(2,128)(2,1)}), bf16[8,2,1280]{2,1,0:T(2,128)(2,1)S(1)}, u32[]{:S(2)}, u32[]{:S(2)}) %all-to-all-start) | async-done | bytes 40992 | tf_op jit(solution)/shard_map/all_to_all | solution.py:17
  54.8 3.3 %all-to-all-start.2 = ((bf16[8,2,1280]{2,1,0:T(2,128)(2,1)}), bf16[8,2,1280]{2,1,0:T(2,128)(2,1)S(1)}, u32[]{:S(2)}, u32[]{:S(2)}) async-start(bf16[8,2,1280]{2,1,0:T(2,128)(2,1)} %reshape.50), calls=%async_computation.2 | async-start | bytes 81920 | tf_op jit(solution)/shard_map/all_to_all | solution.py:17
  58.2 0.0 all-reduce.9.cloned.1.call-start
  58.3 0.0 copy-done
  58.3 1.3 fusion.36
  59.6 5.3 %all-to-all-done.2 = bf16[8,2,1280]{2,1,0:T(2,128)(2,1)S(1)} async-done(((bf16[8,2,1280]{2,1,0:T(2,128)(2,1)}), bf16[8,2,1280]{2,1,0:T(2,128)(2,1)S(1)}, u32[]{:S(2)}, u32[]{:S(2)}) %all-to-all-start.2) | async-done | bytes 40992 | tf_op jit(solution)/shard_map/all_to_all | solution.py:17
  64.9 2.9 %fusion.16 = bf16[16,1280]{1,0:T(8,128)(2,1)S(1)} fusion(bf16[1,1280,1280]{2,1,0:T(8,128)(2,1)} %param.8, f32[16,1280]{1,0:T(8,128)} %get-tuple-element.17, bf16[1,16,1280]{2,0,1:T(2,128)(2,1)S(1)} %bitcast.86), kind=kOutput, calls=%fused_computation.21 | convolution fusion | flops 52633600 | bytes 3440640 | tf_op jit(solution)/shard_map/dot_general | solution.py:57
  67.9 1.6 fusion.22
  69.5 0.8 dot_general.54
  70.3 3.1 %fusion.19 = bf16[8,2,1280]{2,0,1:T(8,128)(2,1)} fusion(bf16[1,1280,1280]{2,1,0:T(8,128)(2,1)} %param.8, bf16[8,2,1280]{2,1,0:T(2,128)(2,1)S(1)} %dot_general.54), kind=kOutput, calls=%fused_computation.22 | convolution fusion | flops 52449280 | bytes 3358720 | tf_op jit(solution)/shard_map/dot_general | solution.py:46
  73.4 0.0 all-reduce.9.cloned.1.call-update
  73.4 2.8 %fusion = bf16[1,1280,1280]{2,1,0:T(8,128)(2,1)} fusion(bf16[16,1280]{1,0:T(8,128)(2,1)S(1)} %fusion.16, bf16[1,16,1280]{2,0,1:T(2,128)(2,1)S(1)} %bitcast.89), kind=kOutput, calls=%fused_computation.2 | convolution fusion | flops 54067200 | bytes 3358720 | tf_op jit(solution)/shard_map/dot_general | solution.py:64
  76.2 0.0 copy-start.9
  76.2 24.5 %all-reduce.9.cloned.1.call-done = (bf16[8,2,1280]{2,0,1:T(8,128)(2,1)}, bf16[8,2,1280]{2,0,1:T(8,128)(2,1)}) async-done(((bf16[8,2,1280]{2,0,1:T(8,128)(2,1)}, bf16[8,2,1280]{2,0,1:T(8,128)(2,1)}), (bf16[8,2,1280]{2,0,1:T(8,128)(2,1)}, bf16[8,2,1280]{2,0,1:T(8,128)(2,1)})) %all-reduce.9.cloned.1.call-update) | async-done | bytes 81936 | tf_op jit(solution)/shard_map/psum | solution.py:21
  100.7 1.4 copy.27
  102.2 5.6 %all-to-all-start.3 = ((bf16[8,2,1280]{2,1,0:T(2,128)(2,1)}), bf16[8,2,1280]{2,1,0:T(2,128)(2,1)S(1)}, u32[]{:S(2)}, u32[]{:S(2)}) async-start(bf16[8,2,1280]{2,1,0:T(2,128)(2,1)} %copy.27), calls=%async_computation.3 | async-start | bytes 81920 | tf_op jit(solution)/shard_map/all_to_all | solution.py:22
  107.8 3.5 %fusion.1 = bf16[1,1280,1280]{2,1,0:T(8,128)(2,1)} fusion(bf16[16,1280]{1,0:T(8,128)(2,1)} %get-tuple-element.16, bf16[1,16,1280]{2,0,1:T(2,128)(2,1)S(1)} %bitcast.87), kind=kOutput, calls=%fused_computation.3 | convolution fusion | flops 54067200 | bytes 3358720 | tf_op jit(solution)/shard_map/dot_general | solution.py:61
  111.3 0.0 copy-done.7
  111.3 0.6 copy.24
  112.0 2.5 all-to-all-done.3
  114.5 3.5 %all-to-all-start.1 = ((bf16[8,2,1280]{2,1,0:T(2,128)(2,1)}), bf16[8,2,1280]{2,1,0:T(2,128)(2,1)S(1)}, u32[]{:S(2)}, u32[]{:S(2)}) async-start(bf16[8,2,1280]{2,1,0:T(2,128)(2,1)} %copy.24), calls=%async_computation.1 | async-start | bytes 81920 | tf_op jit(solution)/shard_map/all_to_all | solution.py:22
  118.0 0.0 all-reduce.7.cloned.1.call-start
  118.0 0.0 copy-done.9
  118.0 0.0 copy-done.11
  118.0 0.0 copy-start.1
  118.1 2.1 fusion.62
  120.2 0.0 copy-done.1
  120.2 0.4 fusion.29
  120.6 4.1 %all-to-all-done.1 = bf16[8,2,1280]{2,1,0:T(2,128)(2,1)S(1)} async-done(((bf16[8,2,1280]{2,1,0:T(2,128)(2,1)}), bf16[8,2,1280]{2,1,0:T(2,128)(2,1)S(1)}, u32[]{:S(2)}, u32[]{:S(2)}) %all-to-all-start.1) | async-done | bytes 40992 | tf_op jit(solution)/shard_map/all_to_all | solution.py:22
  124.7 0.0 copy-done.4
  124.7 0.0 copy-done.6
  124.7 1.9 multiply_reduce_fusion.1
  126.6 5.7 %psum.47 = f32[16]{0:T(128)S(1)} all-reduce(f32[16]{0:T(128)S(1)} %get-tuple-element.6), channel_id=1, replica_groups=mesh['seq'=4,'exp'=8] {'seq'}, use_global_device_ids=true, to_apply=%region_12.0 | all-reduce | flops 16 | bytes 128 | tf_op jit(solution)/shard_map/psum | solution.py:74
  132.3 2.3 convolution_bitcast_fusion
  134.6 0.0 all-reduce.7.cloned.1.call-update
  134.6 0.0 copy-done.2
  134.6 3.4 %fusion.11 = bf16[1,512,1280]{2,1,0:T(8,128)(2,1)} fusion(f32[512,1280]{1,0:T(8,128)} %fusion.62, bf16[1280,16]{0,1:T(8,128)(2,1)S(1)} %copy-done.2, f32[16,512]{1,0:T(8,128)S(1)} %fusion.29, f32[16,512]{1,0:T(8,128)S(1)} %get-tuple-element.18, f32[16]{0:T(128)S(1)} %psum.47, f32[512]{0:T(512)S(1)} %get-tuple-element.5, f32[512]{0:T(512)S(1)} %copy-done.6, ...), kind=kOutput, calls=%fused_computation.15 | convolution fusion | flops 22364160 | bytes 4077760 | tf_op jit(solution)/shard_map/dot_general | solution.py:83
  138.0 1.6 fusion.12
  139.6 112.6 %all-reduce.7.cloned.1.call-done = f32[1280,16]{0,1:T(8,128)} async-done(((f32[1280,16]{0,1:T(8,128)}), f32[1280,16]{0,1:T(8,128)}) %all-reduce.7.cloned.1.call-update) | async-done | bytes 81936
  252.3 1.4 constant_dynamic-slice_fusion
  (10 shorter events, 0.1 us)
Async XLA Ops:
  7.2 51.1 %copy-start = (bf16[1,1280,1280]{2,1,0:T(8,128)(2,1)S(1)}, bf16[1,1280,1280]{2,1,0:T(8,128)(2,1)}, u32[]{:S(2)}) copy-start(bf16[1,1280,1280]{2,1,0:T(8,128)(2,1)} %param.7) | copy-start | bytes 9830404
  9.2 10.8 %copy-start.3 = (f32[512]{0:T(512)}, f32[512]{0:T(512)S(1)}, u32[]{:S(2)}) copy-start(f32[512]{0:T(512)S(1)} %get-tuple-element.9) | copy-start | bytes 6148
  17.6 8.1 %copy-start.8 = (f32[16]{0:T(128)}, f32[16]{0:T(128)S(1)}, u32[]{:S(2)}) copy-start(f32[16]{0:T(128)S(1)} %pmax.7) | copy-start | bytes 196
  17.8 0.6 copy-start.5
  25.7 0.6 copy-start.10
  42.1 12.7 %all-to-all-start = ((bf16[8,2,1280]{2,1,0:T(2,128)(2,1)}), bf16[8,2,1280]{2,1,0:T(2,128)(2,1)S(1)}, u32[]{:S(2)}, u32[]{:S(2)}) async-start(bf16[8,2,1280]{2,1,0:T(2,128)(2,1)} %reshape.48), calls=%async_computation | async-start | bytes 81920 | tf_op jit(solution)/shard_map/all_to_all | solution.py:17
  54.8 10.0 %all-to-all-start.2 = ((bf16[8,2,1280]{2,1,0:T(2,128)(2,1)}), bf16[8,2,1280]{2,1,0:T(2,128)(2,1)S(1)}, u32[]{:S(2)}, u32[]{:S(2)}) async-start(bf16[8,2,1280]{2,1,0:T(2,128)(2,1)} %reshape.50), calls=%async_computation.2 | async-start | bytes 81920 | tf_op jit(solution)/shard_map/all_to_all | solution.py:17
  58.2 42.5 %all-reduce.9.cloned.1.call-start = ((), (), s32[]{:S(2)}) async-start(), calls=%async_computation.5 | async-start | bytes 163840 | tf_op jit(solution)/shard_map/psum | solution.py:21
  76.2 41.9 %copy-start.9 = (f32[16]{0:T(128)S(1)}, f32[16]{0:T(128)}, u32[]{:S(2)}) copy-start(f32[16]{0:T(128)} %copy-done.8) | copy-start | bytes 196
  76.2 41.9 %copy-start.11 = (f32[16]{0:T(128)S(1)}, f32[16]{0:T(128)}, u32[]{:S(2)}) copy-start(f32[16]{0:T(128)} %copy-done.10) | copy-start | bytes 196
  100.7 10.6 %copy-start.7 = (bf16[8,2,1280]{2,0,1:T(8,128)(2,1)S(1)}, bf16[8,2,1280]{2,0,1:T(8,128)(2,1)}, u32[]{:S(2)}) copy-start(bf16[8,2,1280]{2,0,1:T(8,128)(2,1)} %get-tuple-element.13) | copy-start | bytes 122884
  102.2 12.3 %all-to-all-start.3 = ((bf16[8,2,1280]{2,1,0:T(2,128)(2,1)}), bf16[8,2,1280]{2,1,0:T(2,128)(2,1)S(1)}, u32[]{:S(2)}, u32[]{:S(2)}) async-start(bf16[8,2,1280]{2,1,0:T(2,128)(2,1)} %copy.27), calls=%async_computation.3 | async-start | bytes 81920 | tf_op jit(solution)/shard_map/all_to_all | solution.py:22
  111.3 13.4 %copy-start.4 = (f32[512]{0:T(512)S(1)}, f32[512]{0:T(512)}, u32[]{:S(2)}) copy-start(f32[512]{0:T(512)} %copy-done.3) | copy-start | bytes 6148
  111.3 13.4 %copy-start.6 = (f32[512]{0:T(512)S(1)}, f32[512]{0:T(512)}, u32[]{:S(2)}) copy-start(f32[512]{0:T(512)} %copy-done.5) | copy-start | bytes 6148
  114.5 10.2 %all-to-all-start.1 = ((bf16[8,2,1280]{2,1,0:T(2,128)(2,1)}), bf16[8,2,1280]{2,1,0:T(2,128)(2,1)S(1)}, u32[]{:S(2)}, u32[]{:S(2)}) async-start(bf16[8,2,1280]{2,1,0:T(2,128)(2,1)} %copy.24), calls=%async_computation.1 | async-start | bytes 81920 | tf_op jit(solution)/shard_map/all_to_all | solution.py:22
  118.0 134.3 %all-reduce.7.cloned.1.call-start = ((), (), s32[]{:S(2)}) async-start(), calls=%async_computation.4 | async-start | bytes 163840
  118.0 2.1 copy-start.1
  120.2 14.4 %copy-start.2 = (bf16[1280,16]{0,1:T(8,128)(2,1)S(1)}, bf16[1280,16]{0,1:T(8,128)(2,1)}, u32[]{:S(2)}) copy-start(bf16[1280,16]{0,1:T(8,128)(2,1)} %param.6) | copy-start | bytes 122884
Sparse Core Ops, SparseCore 0:
  73.5 27.1 all-reduce.8
  134.7 117.4 all-reduce.6
where the time goes:
time: 263 us; the launch traced here: 260 us
  waiting for transfers between devices  154 us (59%)
  matrix products  32.2 us (12%)
  blocking collectives  31.8 us (12%)
  starting transfers between devices  18.5 us (7%)
  between operations  14.2 us (5%)
  local copies, waits for them, and re-layouts  7.52 us (3%)
    unnamed x3, waiting for transfers between devices  113 us
    psum x1, waiting for transfers between devices, from_experts(): summed = lax.psum(partial_value.astype(jnp.bfloat16), 'seq')  24.5 us
    psum x1, blocking collectives, to_experts(): summed = lax.psum(partial_value, 'seq').astype(jnp.bfloat16)  12.1 us
    all_to_all x2, waiting for transfers between devices, to_experts(): lax.all_to_all(summed, 'exp', split_axis=1, concat_axis=0, tiled=True)  10.5 us
    all_to_all x2, starting transfers between devices, to_experts(): lax.all_to_all(summed, 'exp', split_axis=1, concat_axis=0, tiled=True)  9.33 us
    all_to_all x2, starting transfers between devices, from_experts(): lax.all_to_all(summed, 'exp', split_axis=0, concat_axis=1, tiled=True)  9.06 us
    pmax x1, blocking collectives, shards(): col_top = lax.pmax(jnp.max(logits, axis=1), 'seq')  8.37 us
    all_to_all x2, waiting for transfers between devices, from_experts(): lax.all_to_all(summed, 'exp', split_axis=0, concat_axis=1, tiled=True)  6.63 us
  transfers between devices with their start and end apart: 6, of which 6 were waited for; matrix products, arithmetic and copies ran while one was open for 7% of the time, Pallas kernels for 0%

commit v1 on v0

v1 whole, which is shorter than its diff:
```python
import functools
import math

import jax
import jax.numpy as jnp
from jax import lax
from jax.experimental import pallas as pl
from jax.experimental.pallas import tpu as pltpu
from jax.sharding import PartitionSpec as P

F32 = jnp.float32
BF16 = jnp.bfloat16
LANES = 128
FIRST_FLOPS = 1 << 40
PACK_MIB = 8
EXPERT_MIB = 24
PACK_FLOPS = 1 << 36
OUTER_FLOPS = 1 << 36
VMEM = pl.BlockSpec(memory_space=pltpu.VMEM)
HBM = pl.BlockSpec(memory_space=pltpu.HBM)


def dot(a, b, ca, cb):
    return lax.dot_general(a, b, (((ca,), (cb,)), ((), ())), preferred_element_type=F32)


def pieces(x):
    hi = x.astype(BF16)
    rest = x - hi.astype(F32)
    mid = rest.astype(BF16)
    return hi, mid, (rest - mid.astype(F32)).astype(BF16)


ERFC = (
    0.17087277, -0.82215223, 1.48851587, -1.13520398, 0.27886807,
    -0.18628806, 0.09678418, 0.37409196, 1.00002368, -1.26551223,
)


def gelu_parts(h):
    z = jnp.abs(h) * math.sqrt(0.5)
    t = 1.0 / (1.0 + 0.5 * z)
    poly = jnp.full_like(t, ERFC[0])
    for coefficient in ERFC[1:]:
        poly = poly * t + coefficient
    tail = 0.5 * t * jnp.exp(poly - z * z)
    cdf = jnp.where(h < 0, tail, 1.0 - tail)
    pdf = jnp.exp(-0.5 * h * h) * (1.0 / math.sqrt(2.0 * math.pi))
    return h * cdf, cdf + h * pdf


def call(body, out, vmem_mib, flops, nbytes, scratch=(), in_hbm=(), out_hbm=()):
    def run(*args):
        specs = [HBM if n in in_hbm else VMEM for n in range(len(args))]
        return pl.pallas_call(
            body,
            out_shape=tuple(jax.ShapeDtypeStruct(s, d) for s, d in out),
            in_specs=specs,
            out_specs=tuple(HBM if n in out_hbm else VMEM for n in range(len(out))),
            scratch_shapes=list(scratch),
            compiler_params=pltpu.CompilerParams(vmem_limit_bytes=int(vmem_mib * 2**20)),
            cost_estimate=pl.CostEstimate(flops=flops, bytes_accessed=nbytes, transcendentals=0),
        )(*args)

    return run


def shards(ns, ne, tokens, router, w_in, w_out, grad_out):
    feats, cotangent, w1, w2 = tokens[0], grad_out[0], w_in[0], w_out[0]
    length, width = feats.shape
    slots = router.shape[1]
    per = slots // ne
    hidden_part = w1.shape[1]
    half = width // 2
    wide = width + LANES
    cut = width // (ns * ne)

    def to_seq(x, k):
        return lax.ppermute(x, "seq", [(i, i ^ k) for i in range(ns)])

    def to_all(x):
        return lax.all_to_all(x, ("seq", "exp"), 0, 0, tiled=True)

    def pairs_of(a, b, n):
        at = slice(n * per, (n + 1) * per)
        return jnp.concatenate([a[at], b[at]], axis=0).astype(BF16)

    def stat_tile(*columns):
        lane = lax.broadcasted_iota(jnp.int32, (slots, LANES), 1)
        tile = jnp.zeros((slots, LANES), F32)
        for n, v in enumerate(columns):
            tile = jnp.where(lane == n, v.astype(F32), tile)
        return tile

    def first_kernel(out_ref):
        out_ref[...] = jnp.zeros((8, LANES), F32)

    (begun,) = call(first_kernel, [((8, LANES), F32)], 8, FIRST_FLOPS, 0)()

    def start_kernel(x_ref, r_ref, g_ref, _, part_ref, keep_ref, half_ref):
        x = x_ref[...]
        logits = dot(r_ref[...], x, 1, 1)
        top = jnp.max(logits, axis=1, keepdims=True)
        p = jnp.exp(logits - top)
        p_b = p.astype(BF16)
        total = jnp.sum(p, axis=1, keepdims=True)
        total_b = jnp.sum(p_b.astype(F32), axis=1, keepdims=True)
        e = jnp.exp(logits - jnp.max(logits, axis=0, keepdims=True))
        combine_b = (e / jnp.sum(e, axis=0, keepdims=True)).astype(BF16)
        a = dot(p_b, x, 1, 0)
        b = dot(combine_b, g_ref[...], 1, 0)
        part_ref[:, :width] = a
        part_ref[:, width:wide] = stat_tile(top, total, total_b)
        half_ref[0] = b[:, :half]
        half_ref[1] = b[:, half:]
        core = lax.rem(lax.axis_index("seq"), 2)
        part_ref[:, wide:] = half_ref[1 - core]
        keep_ref[...] = half_ref[core]

    part, keep = call(
        start_kernel,
        [((slots, wide + half), F32), ((slots, half), F32)],
        24,
        6 * slots * length * width,
        4 * length * width,
        [pltpu.VMEM((2, slots, half), F32)],
        in_hbm=(3,),
    )(feats, router.T, cotangent, begun)

    def merged(l_ref, r_ref):
        tops, totals, totals_b = (
            [r[:, width + n : width + n + 1] for r in (l_ref, r_ref)] for n in range(3)
        )
        top = jnp.maximum(*tops)
        scale = [jnp.exp(m - top) for m in tops]
        total, total_b = (scale[0] * v[0] + scale[1] * v[1] for v in (totals, totals_b))
        return scale[0] * l_ref[:, :width] + scale[1] * r_ref[:, :width], top, total, total_b

    def pack_kernel(l_ref, r_ref, keep_ref, part_ref, send_ref, half_ref):
        a, top, total, total_b = merged(l_ref, r_ref)
        part_ref[:, :width] = a
        part_ref[:, width:] = stat_tile(top, total, total_b)
        half_ref[0] = a[:, :half]
        half_ref[1] = a[:, half:]
        a = half_ref[lax.rem(lax.axis_index("seq"), 2)]
        b = keep_ref[...] + r_ref[:, wide:]
        a = jnp.concatenate([a, stat_tile(*pieces(top), *pieces(total_b))], axis=1)
        b = jnp.concatenate([b, jnp.zeros((slots, LANES), F32)], axis=1)
        for e in range(ne):
            chunk = pairs_of(a, b, e)
            for s in range(ns):
                send_ref[s * ne + e] = chunk

    part, send = call(
        pack_kernel,
        [((slots, wide), F32), ((ns * ne, 2 * per, half + LANES), BF16)],
        PACK_MIB,
        PACK_FLOPS,
        8 * slots * wide,
        [pltpu.VMEM((2, slots, half), F32)],
    )(part, to_seq(part, 1), keep)
    rows_in = to_all(send)

    def expert_kernel(*refs):
        w2_ref, in_ref, w1_ref, x_ref, dy_ref, act_ref, dh_ref, out_ref, keep_ref, *scratch = refs
        (half_ref,) = scratch
        tops, totals = [], []
        for s in range(0, ns, 2):
            tile = jnp.concatenate(
                [in_ref[s * ne + c, :, half:].astype(F32)[:per] for c in range(ne)], axis=0
            )
            tops.append(tile[:, 0:1] + tile[:, 1:2] + tile[:, 2:3])
            totals.append(tile[:, 3:4] + tile[:, 4:5] + tile[:, 5:6])
        top = functools.reduce(jnp.maximum, tops)
        scale = [jnp.exp(m - top) for m in tops]
        total = sum(w * v for w, v in zip(scale, totals))
        scale = [w / total for w in scale]
        xs, dys = [[], []], [[], []]
        for core in range(2):
            for c in range(ne):
                at = slice(c * per, (c + 1) * per)
                x, dy = 0.0, 0.0
                for w, s in zip(scale, range(core, ns, 2)):
                    v = in_ref[s * ne + c, :, :half].astype(F32)
                    x += w[at] * v[:per]
                    dy += v[per:]
                xs[core].append(x)
                dys[core].append(dy)
        x, dy = (
            jnp.concatenate([jnp.concatenate(v, axis=0) for v in side], axis=1).astype(BF16)
            for side in (xs, dys)
        )
        x_ref[...] = x
        dy_ref[...] = dy
        w2v = w2_ref[...]
        d_act = dot(dy, w2v, 1, 1)
        act, slope = gelu_parts(dot(x, w1_ref[...], 1, 0))
        act = act.astype(BF16)
        act_ref[...] = act
        dh = (d_act * slope).astype(BF16)
        dh_ref[...] = dh
        y = dot(act, w2v, 1, 0)
        dx = dot(dh, w1_ref[...], 1, 1)
        for core in range(2):
            at = slice(core * half, (core + 1) * half)
            half_ref[core, :slots] = y[:, at]
            half_ref[core, slots:] = dx[:, at]
        core = lax.rem(lax.axis_index("seq"), 2)
        out_ref[...] = half_ref[1 - core]
        keep_ref[...] = half_ref[core]

    x_rows, dy_rows, act, dh, out, keep = call(
        expert_kernel,
        [((slots, width), BF16)] * 2
        + [((slots, hidden_part), BF16)] * 2
        + [((2 * slots, half), F32)] * 2,
        EXPERT_MIB,
        8 * slots * width * hidden_part,
        4 * width * hidden_part,
        [
            pltpu.VMEM((2, 2 * slots, half), F32),
        ],
    )(w2, rows_in, w1)

    def pack_back_kernel(l_ref, r_ref, send_hbm, near_ref, sems):
        full = l_ref[...] + r_ref[...]
        for c in range(ne):
            near_ref[c] = pairs_of(full[:slots], full[slots:], c)
        copies = [
            pltpu.make_async_copy(near_ref, send_hbm.at[pl.ds(s * ne, ne)], sems.at[s]) for s in range(ns)
        ]
        for copy in copies:
            copy.start()
        for copy in copies:
            copy.wait()

    (send,) = call(
        pack_back_kernel,
        [((ns * ne, 2 * per, half), BF16)],
        PACK_MIB,
        2 * slots * width,
        8 * slots * width,
        [pltpu.VMEM((ne, 2 * per, half), BF16), pltpu.SemaphoreType.DMA((ns,))],
        out_hbm=(0,),
    )(keep, to_seq(out, 1))
    rows_back = to_all(send)

    def outer(steps, build, shapes, *operands):
        def body(*refs):
            ins, outs, done_ref, near, sems = refs[:-6], refs[-6:-4], refs[-4], refs[-3:-1], refs[-1]
            pairs = build(*[r[...] for r in ins])
            copies = []
            for n in range(steps):
                for m, (left, right) in enumerate(pairs):
                    step = near[m].shape[0] // steps
                    at = slice(n * step, (n + 1) * step)
                    near[m][at] = dot(left[:, at], right, 0, 0).astype(BF16)
                    copy = pltpu.make_async_copy(near[m].at[at], outs[m].at[at], sems.at[2 * n + m])
                    copy.start()
                    copies.append(copy)
            done_ref[...] = jnp.zeros((8, LANES), F32)
            for copy in copies:
                copy.wait()

        return call(
            body,
            [(shape, BF16) for shape in shapes] + [((8, LANES), F32)],
            16,
            OUTER_FLOPS,
            sum(2 * m * n for m, n in shapes),
            [pltpu.VMEM(shape, BF16) for shape in shapes] + [pltpu.SemaphoreType.DMA((2 * steps,))],
            out_hbm=(0, 1),
        )(*operands)

    d_w_out, d_w_in, written = outer(
        5,
        lambda act, dy, x, dh: ((act, dy), (x, dh)),
        ((hidden_part, width), (width, hidden_part)),
        act,
        dy_rows,
        x_rows,
        dh,
    )

    def merge_kernel(l_ref, r_ref, out_ref):
        a, *stats = merged(l_ref, r_ref)
        out_ref[:, :width] = a
        out_ref[:, width:] = stat_tile(*stats)

    bits = (ns - 1).bit_length()
    for bit in range(1, bits - 1):
        (part,) = call(
            merge_kernel, [((slots, wide), F32)], 8, 4 * slots * width, 12 * slots * width
        )(part, to_seq(part, 1 << bit))

    def softmax_kernel(_, l_ref, r_ref, route_ref, x_ref, row_ref, combine_ref, dispatch_ref):
        a, top, total, total_b = merged(l_ref, r_ref)
        row_ref[...] = a / total_b
        logits = dot(route_ref[...], x_ref[...], 1, 1)
        e = jnp.exp(logits - jnp.max(logits, axis=0, keepdims=True))
        combine_ref[...] = e / jnp.sum(e, axis=0, keepdims=True)
        dispatch_ref[...] = jnp.exp(logits - top) / total

    clip_rows, combine, dispatch = call(
        softmax_kernel,
        [((slots, width), F32), ((slots, length), F32), ((slots, length), F32)],
        8,
        2 * slots * length * width,
        2 * length * width,
        in_hbm=(0,),
    )(written, part, to_seq(part, 1 << (bits - 1)), router.T, feats)

    def logit_kernel(in_ref, a_ref, c_ref, d_ref, x_ref, g_ref, l_ref, y_ref, dx_ref, out):
        y, dx = [], []
        for core in range(2):
            got = [sum(in_ref[s * ne + e].astype(F32) for s in range(core, ns, 2)) for e in range(ne)]
            y.append(jnp.concatenate([v[:per] for v in got], axis=0))
            dx.append(jnp.concatenate([v[per:] for v in got], axis=0))
        y, dx = (jnp.concatenate(v, axis=1).astype(BF16) for v in (y, dx))
        dxf = dx.astype(F32)
        inner = jnp.sum(dxf * a_ref[...], axis=1, keepdims=True)
        x = x_ref[...]
        combine = c_ref[...]
        dispatch = d_ref[...]
        d_combine = dot(y, g_ref[...], 1, 1)
        d_c = combine * (d_combine - jnp.sum(combine * d_combine, axis=0, keepdims=True))
        d_d = dispatch * (dot(dx, x, 1, 1) - inner)
        d_logit = (d_c + d_d).astype(BF16)
        d_route = dot(d_logit, x, 1, 0)
        l_ref[...] = d_logit
        y_ref[...] = y
        dx_ref[...] = dx
        for k in range(ns * ne):
            piece = d_route[:, k * cut : (k + 1) * cut]
            out[k] = jnp.concatenate([piece[: slots // 2], piece[slots // 2 :]], axis=1).astype(BF16)

    d_logit, y, dx, send = call(
        logit_kernel,
        [
            ((slots, length), BF16),
            ((slots, width), BF16),
            ((slots, width), BF16),
            ((ns * ne, slots // 2, 2 * cut), BF16),
        ],
        24,
        6 * slots * length * width,
        4 * length * width,
    )(rows_back, clip_rows, combine, dispatch, feats, cotangent)
    chunks = to_all(send)

    def token_products(combine, dispatch, d_logit, y, dx, route):
        left = jnp.concatenate([dispatch, d_logit.astype(F32)], axis=0).astype(BF16)
        right = jnp.concatenate([dx.astype(F32), route.astype(F32)], axis=0).astype(BF16)
        return (combine.astype(BF16), y), (left, right)

    mixed, d_feats, _ = outer(
        4, token_products, ((length, width),) * 2, combine, dispatch, d_logit, y, dx, router.T
    )

    def sum_kernel(in_ref, out_ref):
        full = jnp.sum(in_ref[...].astype(F32), axis=0)
        out_ref[...] = jnp.concatenate([full[:, :cut], full[:, cut:]], axis=0)

    (d_router,) = call(
        sum_kernel, [((slots, cut), F32)], 8, slots * width, slots * width * 4
    )(chunks)
    return mixed[None], d_feats[None], d_router.T, d_w_in[None], d_w_out[None]


def solution(mesh):
    in_specs = (
        P("exp", "seq", None),
        P(),
        P("exp", None, "seq"),
        P("exp", "seq", None),
        P("exp", "seq", None),
    )
    out_specs = (
        P("exp", "seq", None),
        P("exp", "seq", None),
        P(("seq", "exp"), None),
        P("exp", None, "seq"),
        P("exp", "seq", None),
    )
    body = functools.partial(shards, mesh.shape["seq"], mesh.shape["exp"])
    return jax.shard_map(body, mesh=mesh, in_specs=in_specs, out_specs=out_specs, check_vma=False)
```

time: 263 us -> 49.5 us (0.19)
  waiting for transfers between devices: 154 us -> 10 us
  matrix products: 32.2 us -> 0 us
  blocking collectives: 31.8 us -> 15.6 us
  between operations: 14.2 us -> 0.73 us
  Pallas kernels: 0 us -> 13.3 us
  starting transfers between devices: 18.5 us -> 7.98 us
  local copies, waits for them, and re-layouts: 7.52 us -> 1.69 us
    unnamed x3 -> x0, waiting for transfers between devices: 113 us -> none
    dot_general x15 -> x0, matrix products: 32.2 us -> none  [the longest x1 3.54 us: shards(): lax.dot_general(activated, d_rows, (((0,), (0,)), ((), ())), preferred_el...]
    psum x1 -> x0, waiting for transfers between devices: 24.5 us -> none  [from_experts(): summed = lax.psum(partial_value.astype(jnp.bfloat16), 'seq')]
    psum x3 -> x0, blocking collectives: 23.5 us -> none  [the longest x1 12.1 us: to_experts(): summed = lax.psum(partial_value, 'seq').astype(jnp.bfloat16)]
    all_to_all x0 -> x1, blocking collectives: none -> 15.6 us  [to_all(): return lax.all_to_all(x, ('seq', 'exp'), 0, 0, tiled=True)]
    pallas_call x0 -> x10, Pallas kernels: none -> 13.3 us  [run(): pl.pallas_call(body, out_shape=tuple((jax.ShapeDtypeStruct(s, d) for s, d...]
    all_to_all x4 -> x2, starting transfers between devices: 18.4 us -> 5.83 us  [to_all(): return lax.all_to_all(x, ('seq', 'exp'), 0, 0, tiled=True)]
    pmax x1 -> x0, blocking collectives: 8.37 us -> none  [shards(): col_top = lax.pmax(jnp.max(logits, axis=1), 'seq')]
  transfers between devices with their start and end apart: 6 -> 5, of which waited for: 6 -> 3; matrix products, arithmetic and copies ran while one was open for 7% -> 0% of each run, Pallas kernels for 0% -> 14%
where the time goes in v1:
time: 49.5 us; the launch traced here: 49.3 us
  blocking collectives  15.6 us (32%)
  Pallas kernels  13.3 us (27%)
  waiting for transfers between devices  10 us (20%)
  starting transfers between devices  7.98 us (16%)
  local copies, waits for them, and re-layouts  1.69 us (3%)
  between operations  0.73 us (1%)
    all_to_all x1, blocking collectives, to_all(): return lax.all_to_all(x, ('seq', 'exp'), 0, 0, tiled=True)  15.6 us
    pallas_call x10, Pallas kernels, run(): pl.pallas_call(body, out_shape=tuple((jax.ShapeDtypeStruct(s, d) for s, d...  13.3 us
    all_to_all x2, waiting for transfers between devices, to_all(): return lax.all_to_all(x, ('seq', 'exp'), 0, 0, tiled=True)  9.04 us
    all_to_all x2, starting transfers between devices, to_all(): return lax.all_to_all(x, ('seq', 'exp'), 0, 0, tiled=True)  5.83 us
    ppermute x3, starting transfers between devices, to_seq(): return lax.ppermute(x, 'seq', [(i, i ^ k) for i in range(ns)])  2.15 us
    unnamed x10, local copies, waits for them, and re-layouts  1.69 us
    ppermute x3, waiting for transfers between devices, to_seq(): return lax.ppermute(x, 'seq', [(i, i ^ k) for i in range(ns)])  0.99 us
  transfers between devices with their start and end apart: 5, of which 3 were waited for; matrix products, arithmetic and copies ran while one was open for 0% of the time, Pallas kernels for 14%

profile of v1, /device:TPU:0, one launch (start us, length us, event | category | flops | bytes accessed | tf_op | source)
XLA Modules:
  0.0 49.3 jit_solution(15062770785128296373)
XLA Ops:
  0.6 0.0 copy-start
  0.6 0.0 copy-start.1
  0.7 0.0 copy-start.4
  0.7 1.3 %copy-done = bf16[1,512,1280]{2,1,0:T(8,128)(2,1)S(1)} copy-done((bf16[1,512,1280]{2,1,0:T(8,128)(2,1)S(1)}, bf16[1,512,1280]{2,1,0:T(8,128)(2,1)}, u32[]{:S(2)}) %copy-start) | copy-done | bytes 1310744
  1.9 0.4 copy-done.1
  2.3 0.0 copy-done.4
  2.3 1.0 %shard_map.93 = (f32[16,2048]{1,0:T(8,128)S(1)}, f32[16,640]{1,0:T(8,128)S(1)}) custom-call(bf16[512,1280]{1,0:T(8,128)(2,1)S(1)} %bitcast.10, bf16[16,1280]{1,0:T(8,128)(2,1)S(1)} %bitcast.17, bf16[512,1280]{1,0:T(8,128)(2,1)S(1)} %bitcast.13, f32[8,128]{1,0:T(8,128)S(1)} %shard_map.92._), custom_call_target="tpu_custom_call" | custom-call | flops 62914560 | bytes 2621440 | tf_op jit(solution)/shard_map/pallas_call | solution.py:55
  3.3 0.5 collective-permute-start
  3.8 1.0 %collective-permute-done.r_ref = f32[16,2048]{1,0:T(8,128)S(1)} collective-permute-done((f32[16,2048]{1,0:T(8,128)S(1)}, f32[16,2048]{1,0:T(8,128)S(1)}, u32[]{:S(2)}, u32[]{:S(2)}) %collective-permute-start) | collective-permute-done | bytes 131104 | tf_op jit(solution)/shard_map/ppermute | solution.py:79
  4.8 0.0 copy-start.2
  4.8 0.0 copy-start.3
  4.8 0.2 shard_map.94
  5.0 15.6 %all_to_all.15.refs_1_ = bf16[32,4,768]{2,1,0:T(4,128)(2,1)S(1)} all-to-all(bf16[32,4,768]{2,1,0:T(4,128)(2,1)S(1)} %get-tuple-element.29), channel_id=1, replica_groups=mesh['seq'=4,'exp'=8] {'seq','exp'}, dimensions={0} | all-to-all | bytes 393216 | tf_op jit(solution)/shard_map/all_to_all | solution.py:82
  20.5 0.0 copy-done.2
  20.5 0.0 copy-done.3
  20.5 2.8 %shard_map.95 = (bf16[16,1280]{1,0:T(8,128)(2,1)S(1)}, bf16[16,1280]{1,0:T(8,128)(2,1)S(1)}, bf16[16,1280]{1,0:T(8,128)(2,1)S(1)}, bf16[16,1280]{1,0:T(8,128)(2,...) custom-call(bf16[1280,1280]{1,0:T(8,128)(2,1)S(1)} %bitcast.15, bf16[32,4,768]{2,1,0:T(4,128)(2,1)S(1)} %all_to_all.15.refs_1_, ...), custom_call_target="tpu_custom_call" | custom-call | flops 209715200 | bytes 6553600 | tf_op jit(solution)/shard_map/pallas_call | solution.py:55
  23.4 0.2 collective-permute-start.2
  23.5 1.5 %collective-permute-start.1 = (f32[16,1408]{1,0:T(8,128)S(1)}, f32[16,1408]{1,0:T(8,128)S(1)}, u32[]{:S(2)}, u32[]{:S(2)}) collective-permute-start(f32[16,1408]{1,0:T(8,128)S(1)} %get-tuple-element.35.l_ref), channel_id=1, source_target_pairs={{0,16},{8,24},{16,0},{24,8},{1,17},{9,25},{17,1},{25,9},{2,18},{10... | collective-permute-start | bytes 270344 | tf_op jit(solution)/shard_map/ppermute | solution.py:79
  25.0 0.0 collective-permute-done.2.r_ref
  25.0 0.7 %shard_map.98 = bf16[32,4,640]{2,1,0:T(4,128)(2,1)} custom-call(f32[32,640]{1,0:T(8,128)S(1)} %get-tuple-element.38.l_ref, f32[32,640]{1,0:T(8,128)S(1)} %collective-permute-done.2.r_ref), custom_call_target="tpu_custom_call" | custom-call | flops 40960 | bytes 163840 | tf_op jit(solution)/shard_map/pallas_call | solution.py:55
  25.8 2.8 %all-to-all-start.1 = ((bf16[32,4,640]{2,1,0:T(4,128)(2,1)}), bf16[32,4,640]{2,1,0:T(4,128)(2,1)S(1)}, u32[]{:S(2)}, u32[]{:S(2)}) async-start(bf16[32,4,640]{2,1,0:T(4,128)(2,1)} %shard_map.98), calls=%async_computation.1 | async-start | bytes 327680 | tf_op jit(solution)/shard_map/all_to_all | solution.py:82
  28.6 3.2 %shard_map.96 = (bf16[1280,1280]{1,0:T(8,128)(2,1)}, bf16[1280,1280]{1,0:T(8,128)(2,1)}, f32[8,128]{1,0:T(8,128)S(1)}) custom-call(bf16[16,1280]{1,0:T(8,128)(2,1)S(1)} %get-tuple-element.30.refs_0_, bf16[16,1280]{1,0:T(8,128)(2,1)S(1)} %get-tuple-element.31.refs_1_, bf16[16,1280]{1,0:T(8,128)(2,1)S(1)} %get-tuple-element.32.refs_2_, ...), custom_call_target="tpu_custom_call" | custom-call | flops 68719476736 | bytes 6553600 | tf_op jit(solution)/shard_map/pallas_call | solution.py:55
  31.8 0.0 collective-permute-done.1.r_ref
  31.9 0.5 shard_map.97
  32.3 4.2 %all-to-all-done.1.in_ref = bf16[32,4,640]{2,1,0:T(4,128)(2,1)S(1)} async-done(((bf16[32,4,640]{2,1,0:T(4,128)(2,1)}), bf16[32,4,640]{2,1,0:T(4,128)(2,1)S(1)}, u32[]{:S(2)}, u32[]{:S(2)}) %all-to-all-start.1) | async-done | bytes 163872 | tf_op jit(solution)/shard_map/all_to_all | solution.py:82
  36.5 1.8 %shard_map.99 = (bf16[16,512]{1,0:T(8,128)(2,1)S(1)}, bf16[16,1280]{1,0:T(8,128)(2,1)S(1)}, bf16[16,1280]{1,0:T(8,128)(2,1)S(1)}, bf16[32,8,80]{2,1,0:T(8,128)(2,1)}) custom-call(bf16[32,4,640]{2,1,0:T(4,128)(2,1)S(1)} %all-to-all-done.1.in_ref, f32[16,1280]{1,0:T(8,128)S(1)} %get-tuple-element.40.a_ref, f32[16,512]{1,0:T(8,128)S(1)} %get-tuple-element.36.c_ref.refs_0_, ...), custom_call_target="tpu_custom_call" | custom-call | flops 62914560 | bytes 2621440 | tf_op jit(solution)/shard_map/pallas_call | solution.py:55
  38.3 3.0 %all-to-all-start.2 = ((bf16[32,8,80]{2,1,0:T(8,128)(2,1)}), bf16[32,8,80]{2,1,0:T(8,128)(2,1)S(1)}, u32[]{:S(2)}, u32[]{:S(2)}) async-start(bf16[32,8,80]{2,1,0:T(8,128)(2,1)} %get-tuple-element.46), calls=%async_computation.2 | async-start | bytes 131072 | tf_op jit(solution)/shard_map/all_to_all | solution.py:82
  41.3 2.4 %shard_map.100 = (bf16[512,1280]{1,0:T(8,128)(2,1)}, bf16[512,1280]{1,0:T(8,128)(2,1)}, f32[8,128]{1,0:T(8,128)}) custom-call(f32[16,512]{1,0:T(8,128)S(1)} %get-tuple-element.36.c_ref.refs_0_, f32[16,512]{1,0:T(8,128)S(1)} %get-tuple-element.37.d_ref.refs_1_, bf16[16,512]{1,0:T(8,128)(2,1)S(1)} %get-tuple-element.41.refs_2_, ...), custom_call_target="tpu_custom_call" | custom-call | flops 68719476736 | bytes 2621440 | tf_op jit(solution)/shard_map/pallas_call | solution.py:55
  43.7 4.8 %all-to-all-done.2.in_ref = bf16[32,8,80]{2,1,0:T(8,128)(2,1)S(1)} async-done(((bf16[32,8,80]{2,1,0:T(8,128)(2,1)}), bf16[32,8,80]{2,1,0:T(8,128)(2,1)S(1)}, u32[]{:S(2)}, u32[]{:S(2)}) %all-to-all-start.2) | async-done | bytes 40992 | tf_op jit(solution)/shard_map/all_to_all | solution.py:82
  48.6 0.7 %shard_map.101 = f32[16,40]{1,0:T(8,128)} custom-call(bf16[32,8,80]{2,1,0:T(8,128)(2,1)S(1)} %all-to-all-done.2.in_ref), custom_call_target="tpu_custom_call" | custom-call | flops 20480 | bytes 81920 | tf_op jit(solution)/shard_map/pallas_call | solution.py:55
  (1 shorter events, 0.0 us)
Async XLA Ops:
  0.6 1.3 %copy-start = (bf16[1,512,1280]{2,1,0:T(8,128)(2,1)S(1)}, bf16[1,512,1280]{2,1,0:T(8,128)(2,1)}, u32[]{:S(2)}) copy-start(bf16[1,512,1280]{2,1,0:T(8,128)(2,1)} %param.5) | copy-start | bytes 3932164
  0.6 1.7 %copy-start.1 = (bf16[1,512,1280]{2,1,0:T(8,128)(2,1)S(1)}, bf16[1,512,1280]{2,1,0:T(8,128)(2,1)}, u32[]{:S(2)}) copy-start(bf16[1,512,1280]{2,1,0:T(8,128)(2,1)} %param.9) | copy-start | bytes 3932164
  0.7 1.7 %copy-start.4 = (bf16[1280,16]{0,1:T(8,128)(2,1)S(1)}, bf16[1280,16]{0,1:T(8,128)(2,1)}, u32[]{:S(2)}) copy-start(bf16[1280,16]{0,1:T(8,128)(2,1)} %param.6) | copy-start | bytes 122884
  3.3 1.5 %collective-permute-start = (f32[16,2048]{1,0:T(8,128)S(1)}, f32[16,2048]{1,0:T(8,128)S(1)}, u32[]{:S(2)}, u32[]{:S(2)}) collective-permute-start(f32[16,2048]{1,0:T(8,128)S(1)} %get-tuple-element.27.l_ref), channel_id=1, source_target_pairs={{0,8},{8,0},{16,24},{24,16},{1,9},{9,1},{17,25},{25,17},{2,10},{10... | collective-permute-start | bytes 393224 | tf_op jit(solution)/shard_map/ppermute | solution.py:79
  4.8 15.8 %copy-start.2 = (bf16[1,1280,1280]{2,1,0:T(8,128)(2,1)S(1)}, bf16[1,1280,1280]{2,1,0:T(8,128)(2,1)}, u32[]{:S(2)}) copy-start(bf16[1,1280,1280]{2,1,0:T(8,128)(2,1)} %param.8) | copy-start | bytes 9830404
  4.8 15.8 %copy-start.3 = (bf16[1,1280,1280]{2,1,0:T(8,128)(2,1)S(1)}, bf16[1,1280,1280]{2,1,0:T(8,128)(2,1)}, u32[]{:S(2)}) copy-start(bf16[1,1280,1280]{2,1,0:T(8,128)(2,1)} %param.7) | copy-start | bytes 9830404
  23.4 1.7 %collective-permute-start.2 = (f32[32,640]{1,0:T(8,128)S(1)}, f32[32,640]{1,0:T(8,128)S(1)}, u32[]{:S(2)}, u32[]{:S(2)}) collective-permute-start(f32[32,640]{1,0:T(8,128)S(1)} %get-tuple-element.39), channel_id=1, source_target_pairs={{0,8},{8,0},{16,24},{24,16},{1,9},{9,1},{17,25},{25,17},{2,10},{10... | collective-permute-start | bytes 245768 | tf_op jit(solution)/shard_map/ppermute | solution.py:79
  23.5 8.3 %collective-permute-start.1 = (f32[16,1408]{1,0:T(8,128)S(1)}, f32[16,1408]{1,0:T(8,128)S(1)}, u32[]{:S(2)}, u32[]{:S(2)}) collective-permute-start(f32[16,1408]{1,0:T(8,128)S(1)} %get-tuple-element.35.l_ref), channel_id=1, source_target_pairs={{0,16},{8,24},{16,0},{24,8},{1,17},{9,25},{17,1},{25,9},{2,18},{10... | collective-permute-start | bytes 270344 | tf_op jit(solution)/shard_map/ppermute | solution.py:79
  25.8 10.8 %all-to-all-start.1 = ((bf16[32,4,640]{2,1,0:T(4,128)(2,1)}), bf16[32,4,640]{2,1,0:T(4,128)(2,1)S(1)}, u32[]{:S(2)}, u32[]{:S(2)}) async-start(bf16[32,4,640]{2,1,0:T(4,128)(2,1)} %shard_map.98), calls=%async_computation.1 | async-start | bytes 327680 | tf_op jit(solution)/shard_map/all_to_all | solution.py:82
  38.3 10.3 %all-to-all-start.2 = ((bf16[32,8,80]{2,1,0:T(8,128)(2,1)}), bf16[32,8,80]{2,1,0:T(8,128)(2,1)S(1)}, u32[]{:S(2)}, u32[]{:S(2)}) async-start(bf16[32,8,80]{2,1,0:T(8,128)(2,1)} %get-tuple-element.46), calls=%async_computation.2 | async-start | bytes 131072 | tf_op jit(solution)/shard_map/all_to_all | solution.py:82

commit v2 on v1

--- a/solution.py
+++ b/solution.py
@@ -97,7 +97,7 @@
 
     (begun,) = call(first_kernel, [((8, LANES), F32)], 8, FIRST_FLOPS, 0)()
 
-    def start_kernel(x_ref, r_ref, g_ref, _, part_ref, keep_ref, half_ref):
+    def token_kernel(x_ref, r_ref, _, part_ref, combine_ref):
         x = x_ref[...]
         logits = dot(r_ref[...], x, 1, 1)
         top = jnp.max(logits, axis=1, keepdims=True)
@@ -106,11 +106,22 @@
         total = jnp.sum(p, axis=1, keepdims=True)
         total_b = jnp.sum(p_b.astype(F32), axis=1, keepdims=True)
         e = jnp.exp(logits - jnp.max(logits, axis=0, keepdims=True))
-        combine_b = (e / jnp.sum(e, axis=0, keepdims=True)).astype(BF16)
-        a = dot(p_b, x, 1, 0)
-        b = dot(combine_b, g_ref[...], 1, 0)
-        part_ref[:, :width] = a
-        part_ref[:, width:wide] = stat_tile(top, total, total_b)
+        combine_ref[...] = (e / jnp.sum(e, axis=0, keepdims=True)).astype(BF16)
+        part_ref[:, :width] = dot(p_b, x, 1, 0)
+        part_ref[:, width:] = stat_tile(top, total, total_b)
+
+    part, combine_b = call(
+        token_kernel,
+        [((slots, wide), F32), ((slots, length), BF16)],
+        24,
+        4 * slots * length * width,
+        2 * length * width,
+        in_hbm=(2,),
+    )(feats, router.T, begun)
+
+    def cotangent_kernel(p_ref, c_ref, g_ref, part_ref, keep_ref, half_ref):
+        part_ref[:, :wide] = p_ref[...]
+        b = dot(c_ref[...], g_ref[...], 1, 0)
         half_ref[0] = b[:, :half]
         half_ref[1] = b[:, half:]
         core = lax.rem(lax.axis_index("seq"), 2)
@@ -118,14 +129,13 @@
         keep_ref[...] = half_ref[core]
 
     part, keep = call(
-        start_kernel,
+        cotangent_kernel,
         [((slots, wide + half), F32), ((slots, half), F32)],
         24,
-        6 * slots * length * width,
-        4 * length * width,
+        2 * slots * length * width,
+        2 * length * width,
         [pltpu.VMEM((2, slots, half), F32)],
-        in_hbm=(3,),
-    )(feats, router.T, cotangent, begun)
+    )(part, combine_b, cotangent)
 
     def merged(l_ref, r_ref):
         tops, totals, totals_b = (
@@ -144,16 +154,15 @@
         half_ref[1] = a[:, half:]
         a = half_ref[lax.rem(lax.axis_index("seq"), 2)]
         b = keep_ref[...] + r_ref[:, wide:]
-        a = jnp.concatenate([a, stat_tile(*pieces(top), *pieces(total_b))], axis=1)
-        b = jnp.concatenate([b, jnp.zeros((slots, LANES), F32)], axis=1)
+        rows = jnp.concatenate([a, b, stat_tile(*pieces(top), *pieces(total_b))], axis=1)
         for e in range(ne):
-            chunk = pairs_of(a, b, e)
+            chunk = rows[e * per : (e + 1) * per].astype(BF16)
             for s in range(ns):
                 send_ref[s * ne + e] = chunk
 
     part, send = call(
         pack_kernel,
-        [((slots, wide), F32), ((ns * ne, 2 * per, half + LANES), BF16)],
+        [((slots, wide), F32), ((ns * ne, per, wide), BF16)],
         PACK_MIB,
         PACK_FLOPS,
         8 * slots * wide,
@@ -167,7 +176,7 @@
         tops, totals = [], []
         for s in range(0, ns, 2):
             tile = jnp.concatenate(
-                [in_ref[s * ne + c, :, half:].astype(F32)[:per] for c in range(ne)], axis=0
+                [in_ref[s * ne + c, :, width:].astype(F32) for c in range(ne)], axis=0
             )
             tops.append(tile[:, 0:1] + tile[:, 1:2] + tile[:, 2:3])
             totals.append(tile[:, 3:4] + tile[:, 4:5] + tile[:, 5:6])
@@ -181,9 +190,8 @@
                 at = slice(c * per, (c + 1) * per)
                 x, dy = 0.0, 0.0
                 for w, s in zip(scale, range(core, ns, 2)):
-                    v = in_ref[s * ne + c, :, :half].astype(F32)
-                    x += w[at] * v[:per]
-                    dy += v[per:]
+                    x += w[at] * in_ref[s * ne + c, :, :half].astype(F32)
+                    dy += in_ref[s * ne + c, :, half:width].astype(F32)
                 xs[core].append(x)
                 dys[core].append(dy)
         x, dy = (

time: 49.5 us -> 48.9 us (0.988)
  blocking collectives: 15.6 us -> 15.1 us
    all_to_all x1, blocking collectives: 15.6 us -> 15.1 us  [to_all(): return lax.all_to_all(x, ('seq', 'exp'), 0, 0, tiled=True)]
    pallas_call x10 -> x11, Pallas kernels: 13.3 us -> 13.4 us  [run(): pl.pallas_call(body, out_shape=tuple((jax.ShapeDtypeStruct(s, d) for s, d...]
where the time goes in v2:
time: 48.9 us; the launch traced here: 48.6 us
  blocking collectives  15.1 us (31%)
  Pallas kernels  13.4 us (27%)
  waiting for transfers between devices  10 us (20%)
  starting transfers between devices  8.13 us (17%)
  local copies, waits for them, and re-layouts  1.3 us (3%)
  between operations  0.73 us (1%)
    all_to_all x1, blocking collectives, to_all(): return lax.all_to_all(x, ('seq', 'exp'), 0, 0, tiled=True)  15.1 us
    pallas_call x11, Pallas kernels, run(): pl.pallas_call(body, out_shape=tuple((jax.ShapeDtypeStruct(s, d) for s, d...  13.4 us
    all_to_all x2, waiting for transfers between devices, to_all(): return lax.all_to_all(x, ('seq', 'exp'), 0, 0, tiled=True)  9.04 us
    all_to_all x2, starting transfers between devices, to_all(): return lax.all_to_all(x, ('seq', 'exp'), 0, 0, tiled=True)  5.9 us
    ppermute x3, starting transfers between devices, to_seq(): return lax.ppermute(x, 'seq', [(i, i ^ k) for i in range(ns)])  2.23 us
    unnamed x10, local copies, waits for them, and re-layouts  1.3 us
    ppermute x3, waiting for transfers between devices, to_seq(): return lax.ppermute(x, 'seq', [(i, i ^ k) for i in range(ns)])  0.99 us
  transfers between devices with their start and end apart: 5, of which 3 were waited for; matrix products, arithmetic and copies ran while one was open for 0% of the time, Pallas kernels for 14%

profile of v2, /device:TPU:0, one launch (start us, length us, event | category | flops | bytes accessed | tf_op | source)
XLA Modules:
  0.0 48.6 jit_solution(12117306677582177351)
XLA Ops:
  0.6 0.0 copy-start
  0.6 0.0 copy-start.4
  0.7 0.0 copy-start.1
  0.7 1.3 %copy-done = bf16[1,512,1280]{2,1,0:T(8,128)(2,1)S(1)} copy-done((bf16[1,512,1280]{2,1,0:T(8,128)(2,1)S(1)}, bf16[1,512,1280]{2,1,0:T(8,128)(2,1)}, u32[]{:S(2)}) %copy-start) | copy-done | bytes 1310744
  1.9 0.0 copy-done.4
  2.0 0.8 %shard_map.93 = (f32[16,1408]{1,0:T(8,128)S(1)}, bf16[16,512]{1,0:T(8,128)(2,1)S(1)}) custom-call(bf16[512,1280]{1,0:T(8,128)(2,1)S(1)} %bitcast.10, bf16[16,1280]{1,0:T(8,128)(2,1)S(1)} %bitcast.17, f32[8,128]{1,0:T(8,128)S(1)} %shard_map.92._), custom_call_target="tpu_custom_call" | custom-call | flops 41943040 | bytes 1310720 | tf_op jit(solution)/shard_map/pallas_call | solution.py:55
  2.7 0.0 copy-done.1
  2.7 0.3 shard_map.94
  3.0 0.5 collective-permute-start
  3.5 1.0 %collective-permute-done.r_ref = f32[16,2048]{1,0:T(8,128)S(1)} collective-permute-done((f32[16,2048]{1,0:T(8,128)S(1)}, f32[16,2048]{1,0:T(8,128)S(1)}, u32[]{:S(2)}, u32[]{:S(2)}) %collective-permute-start) | collective-permute-done | bytes 131104 | tf_op jit(solution)/shard_map/ppermute | solution.py:79
  4.5 0.0 copy-start.2
  4.5 0.0 copy-start.3
  4.5 0.2 shard_map.95
  4.7 15.1 %all_to_all.15.refs_1_ = bf16[32,2,1408]{2,1,0:T(2,128)(2,1)S(1)} all-to-all(bf16[32,2,1408]{2,1,0:T(2,128)(2,1)S(1)} %get-tuple-element.33), channel_id=1, replica_groups=mesh['seq'=4,'exp'=8] {'seq','exp'}, dimensions={0} | all-to-all | bytes 360448 | tf_op jit(solution)/shard_map/all_to_all | solution.py:82
  19.7 0.0 copy-done.2
  19.7 0.0 copy-done.3
  19.7 2.8 %shard_map.96 = (bf16[16,1280]{1,0:T(8,128)(2,1)S(1)}, bf16[16,1280]{1,0:T(8,128)(2,1)S(1)}, bf16[16,1280]{1,0:T(8,128)(2,1)S(1)}, bf16[16,1280]{1,0:T(8,128)(2,...) custom-call(bf16[1280,1280]{1,0:T(8,128)(2,1)S(1)} %bitcast.15, bf16[32,2,1408]{2,1,0:T(2,128)(2,1)S(1)} %all_to_all.15.refs_1_, ...), custom_call_target="tpu_custom_call" | custom-call | flops 209715200 | bytes 6553600 | tf_op jit(solution)/shard_map/pallas_call | solution.py:55
  22.6 0.3 collective-permute-start.2
  22.8 1.5 %collective-permute-start.1 = (f32[16,1408]{1,0:T(8,128)S(1)}, f32[16,1408]{1,0:T(8,128)S(1)}, u32[]{:S(2)}, u32[]{:S(2)}) collective-permute-start(f32[16,1408]{1,0:T(8,128)S(1)} %get-tuple-element.39.l_ref), channel_id=1, source_target_pairs={{0,16},{8,24},{16,0},{24,8},{1,17},{9,25},{17,1},{25,9},{2,18},{10... | collective-permute-start | bytes 270344 | tf_op jit(solution)/shard_map/ppermute | solution.py:79
  24.3 0.0 collective-permute-done.2.r_ref
  24.3 0.7 %shard_map.99 = bf16[32,4,640]{2,1,0:T(4,128)(2,1)} custom-call(f32[32,640]{1,0:T(8,128)S(1)} %get-tuple-element.42.l_ref, f32[32,640]{1,0:T(8,128)S(1)} %collective-permute-done.2.r_ref), custom_call_target="tpu_custom_call" | custom-call | flops 40960 | bytes 163840 | tf_op jit(solution)/shard_map/pallas_call | solution.py:55
  25.1 2.9 %all-to-all-start.1 = ((bf16[32,4,640]{2,1,0:T(4,128)(2,1)}), bf16[32,4,640]{2,1,0:T(4,128)(2,1)S(1)}, u32[]{:S(2)}, u32[]{:S(2)}) async-start(bf16[32,4,640]{2,1,0:T(4,128)(2,1)} %shard_map.99), calls=%async_computation.1 | async-start | bytes 327680 | tf_op jit(solution)/shard_map/all_to_all | solution.py:82
  28.0 3.2 %shard_map.97 = (bf16[1280,1280]{1,0:T(8,128)(2,1)}, bf16[1280,1280]{1,0:T(8,128)(2,1)}, f32[8,128]{1,0:T(8,128)S(1)}) custom-call(bf16[16,1280]{1,0:T(8,128)(2,1)S(1)} %get-tuple-element.34.refs_0_, bf16[16,1280]{1,0:T(8,128)(2,1)S(1)} %get-tuple-element.35.refs_1_, bf16[16,1280]{1,0:T(8,128)(2,1)S(1)} %get-tuple-element.36.refs_2_, ...), custom_call_target="tpu_custom_call" | custom-call | flops 68719476736 | bytes 6553600 | tf_op jit(solution)/shard_map/pallas_call | solution.py:55
  31.2 0.0 collective-permute-done.1.r_ref
  31.2 0.5 shard_map.98
  31.7 4.2 %all-to-all-done.1.in_ref = bf16[32,4,640]{2,1,0:T(4,128)(2,1)S(1)} async-done(((bf16[32,4,640]{2,1,0:T(4,128)(2,1)}), bf16[32,4,640]{2,1,0:T(4,128)(2,1)S(1)}, u32[]{:S(2)}, u32[]{:S(2)}) %all-to-all-start.1) | async-done | bytes 163872 | tf_op jit(solution)/shard_map/all_to_all | solution.py:82
  35.9 1.8 %shard_map.100 = (bf16[16,512]{1,0:T(8,128)(2,1)S(1)}, bf16[16,1280]{1,0:T(8,128)(2,1)S(1)}, bf16[16,1280]{1,0:T(8,128)(2,1)S(1)}, bf16[32,8,80]{2,1,0:T(8,128)(2,1)}) custom-call(bf16[32,4,640]{2,1,0:T(4,128)(2,1)S(1)} %all-to-all-done.1.in_ref, f32[16,1280]{1,0:T(8,128)S(1)} %get-tuple-element.44.a_ref, f32[16,512]{1,0:T(8,128)S(1)} %get-tuple-element.40.c_ref.refs_0_, ...), custom_call_target="tpu_custom_call" | custom-call | flops 62914560 | bytes 2621440 | tf_op jit(solution)/shard_map/pallas_call | solution.py:55
  37.7 3.0 %all-to-all-start.2 = ((bf16[32,8,80]{2,1,0:T(8,128)(2,1)}), bf16[32,8,80]{2,1,0:T(8,128)(2,1)S(1)}, u32[]{:S(2)}, u32[]{:S(2)}) async-start(bf16[32,8,80]{2,1,0:T(8,128)(2,1)} %get-tuple-element.50), calls=%async_computation.2 | async-start | bytes 131072 | tf_op jit(solution)/shard_map/all_to_all | solution.py:82
  40.7 2.4 %shard_map.101 = (bf16[512,1280]{1,0:T(8,128)(2,1)}, bf16[512,1280]{1,0:T(8,128)(2,1)}, f32[8,128]{1,0:T(8,128)}) custom-call(f32[16,512]{1,0:T(8,128)S(1)} %get-tuple-element.40.c_ref.refs_0_, f32[16,512]{1,0:T(8,128)S(1)} %get-tuple-element.41.d_ref.refs_1_, bf16[16,512]{1,0:T(8,128)(2,1)S(1)} %get-tuple-element.45.refs_2_, ...), custom_call_target="tpu_custom_call" | custom-call | flops 68719476736 | bytes 2621440 | tf_op jit(solution)/shard_map/pallas_call | solution.py:55
  43.1 4.8 %all-to-all-done.2.in_ref = bf16[32,8,80]{2,1,0:T(8,128)(2,1)S(1)} async-done(((bf16[32,8,80]{2,1,0:T(8,128)(2,1)}), bf16[32,8,80]{2,1,0:T(8,128)(2,1)S(1)}, u32[]{:S(2)}, u32[]{:S(2)}) %all-to-all-start.2) | async-done | bytes 40992 | tf_op jit(solution)/shard_map/all_to_all | solution.py:82
  47.9 0.7 %shard_map.102 = f32[16,40]{1,0:T(8,128)} custom-call(bf16[32,8,80]{2,1,0:T(8,128)(2,1)S(1)} %all-to-all-done.2.in_ref), custom_call_target="tpu_custom_call" | custom-call | flops 20480 | bytes 81920 | tf_op jit(solution)/shard_map/pallas_call | solution.py:55
  (1 shorter events, 0.0 us)
Async XLA Ops:
  0.6 1.3 %copy-start = (bf16[1,512,1280]{2,1,0:T(8,128)(2,1)S(1)}, bf16[1,512,1280]{2,1,0:T(8,128)(2,1)}, u32[]{:S(2)}) copy-start(bf16[1,512,1280]{2,1,0:T(8,128)(2,1)} %param.5) | copy-start | bytes 3932164
  0.6 1.3 %copy-start.4 = (bf16[1280,16]{0,1:T(8,128)(2,1)S(1)}, bf16[1280,16]{0,1:T(8,128)(2,1)}, u32[]{:S(2)}) copy-start(bf16[1280,16]{0,1:T(8,128)(2,1)} %param.6) | copy-start | bytes 122884
  0.7 2.1 %copy-start.1 = (bf16[1,512,1280]{2,1,0:T(8,128)(2,1)S(1)}, bf16[1,512,1280]{2,1,0:T(8,128)(2,1)}, u32[]{:S(2)}) copy-start(bf16[1,512,1280]{2,1,0:T(8,128)(2,1)} %param.9) | copy-start | bytes 3932164
  3.0 1.5 %collective-permute-start = (f32[16,2048]{1,0:T(8,128)S(1)}, f32[16,2048]{1,0:T(8,128)S(1)}, u32[]{:S(2)}, u32[]{:S(2)}) collective-permute-start(f32[16,2048]{1,0:T(8,128)S(1)} %get-tuple-element.31.l_ref), channel_id=1, source_target_pairs={{0,8},{8,0},{16,24},{24,16},{1,9},{9,1},{17,25},{25,17},{2,10},{10... | collective-permute-start | bytes 393224 | tf_op jit(solution)/shard_map/ppermute | solution.py:79
  4.5 15.2 %copy-start.2 = (bf16[1,1280,1280]{2,1,0:T(8,128)(2,1)S(1)}, bf16[1,1280,1280]{2,1,0:T(8,128)(2,1)}, u32[]{:S(2)}) copy-start(bf16[1,1280,1280]{2,1,0:T(8,128)(2,1)} %param.8) | copy-start | bytes 9830404
  4.5 15.2 %copy-start.3 = (bf16[1,1280,1280]{2,1,0:T(8,128)(2,1)S(1)}, bf16[1,1280,1280]{2,1,0:T(8,128)(2,1)}, u32[]{:S(2)}) copy-start(bf16[1,1280,1280]{2,1,0:T(8,128)(2,1)} %param.7) | copy-start | bytes 9830404
  22.6 1.8 %collective-permute-start.2 = (f32[32,640]{1,0:T(8,128)S(1)}, f32[32,640]{1,0:T(8,128)S(1)}, u32[]{:S(2)}, u32[]{:S(2)}) collective-permute-start(f32[32,640]{1,0:T(8,128)S(1)} %get-tuple-element.43), channel_id=1, source_target_pairs={{0,8},{8,0},{16,24},{24,16},{1,9},{9,1},{17,25},{25,17},{2,10},{10... | collective-permute-start | bytes 245768 | tf_op jit(solution)/shard_map/ppermute | solution.py:79
  22.8 8.4 %collective-permute-start.1 = (f32[16,1408]{1,0:T(8,128)S(1)}, f32[16,1408]{1,0:T(8,128)S(1)}, u32[]{:S(2)}, u32[]{:S(2)}) collective-permute-start(f32[16,1408]{1,0:T(8,128)S(1)} %get-tuple-element.39.l_ref), channel_id=1, source_target_pairs={{0,16},{8,24},{16,0},{24,8},{1,17},{9,25},{17,1},{25,9},{2,18},{10... | collective-permute-start | bytes 270344 | tf_op jit(solution)/shard_map/ppermute | solution.py:79
  25.1 10.8 %all-to-all-start.1 = ((bf16[32,4,640]{2,1,0:T(4,128)(2,1)}), bf16[32,4,640]{2,1,0:T(4,128)(2,1)S(1)}, u32[]{:S(2)}, u32[]{:S(2)}) async-start(bf16[32,4,640]{2,1,0:T(4,128)(2,1)} %shard_map.99), calls=%async_computation.1 | async-start | bytes 327680 | tf_op jit(solution)/shard_map/all_to_all | solution.py:82
  37.7 10.3 %all-to-all-start.2 = ((bf16[32,8,80]{2,1,0:T(8,128)(2,1)}), bf16[32,8,80]{2,1,0:T(8,128)(2,1)S(1)}, u32[]{:S(2)}, u32[]{:S(2)}) async-start(bf16[32,8,80]{2,1,0:T(8,128)(2,1)} %get-tuple-element.50), calls=%async_computation.2 | async-start | bytes 131072 | tf_op jit(solution)/shard_map/all_to_all | solution.py:82

commit v3 on v2

--- a/solution.py
+++ b/solution.py
@@ -80,10 +80,6 @@
 
     def to_all(x):
         return lax.all_to_all(x, ("seq", "exp"), 0, 0, tiled=True)
-
-    def pairs_of(a, b, n):
-        at = slice(n * per, (n + 1) * per)
-        return jnp.concatenate([a[at], b[at]], axis=0).astype(BF16)
 
     def stat_tile(*columns):
         lane = lax.broadcasted_iota(jnp.int32, (slots, LANES), 1)
@@ -211,8 +207,8 @@
         dx = dot(dh, w1_ref[...], 1, 1)
         for core in range(2):
             at = slice(core * half, (core + 1) * half)
-            half_ref[core, :slots] = y[:, at]
-            half_ref[core, slots:] = dx[:, at]
+            half_ref[core, :, :half] = y[:, at]
+            half_ref[core, :, half:] = dx[:, at]
         core = lax.rem(lax.axis_index("seq"), 2)
         out_ref[...] = half_ref[1 - core]
         keep_ref[...] = half_ref[core]
@@ -221,35 +217,28 @@
         expert_kernel,
         [((slots, width), BF16)] * 2
         + [((slots, hidden_part), BF16)] * 2
-        + [((2 * slots, half), F32)] * 2,
+        + [((slots, width), F32)] * 2,
         EXPERT_MIB,
         8 * slots * width * hidden_part,
         4 * width * hidden_part,
         [
-            pltpu.VMEM((2, 2 * slots, half), F32),
+            pltpu.VMEM((2, slots, width), F32),
         ],
     )(w2, rows_in, w1)
 
-    def pack_back_kernel(l_ref, r_ref, send_hbm, near_ref, sems):
+    def pack_back_kernel(l_ref, r_ref, send_ref):
         full = l_ref[...] + r_ref[...]
         for c in range(ne):
-            near_ref[c] = pairs_of(full[:slots], full[slots:], c)
-        copies = [
-            pltpu.make_async_copy(near_ref, send_hbm.at[pl.ds(s * ne, ne)], sems.at[s]) for s in range(ns)
-        ]
-        for copy in copies:
-            copy.start()
-        for copy in copies:
-            copy.wait()
+            chunk = full[c * per : (c + 1) * per].astype(BF16)
+            for s in range(ns):
+                send_ref[s * ne + c] = chunk
 
     (send,) = call(
         pack_back_kernel,
-        [((ns * ne, 2 * per, half), BF16)],
+        [((ns * ne, per, width), BF16)],
         PACK_MIB,
         2 * slots * width,
         8 * slots * width,
-        [pltpu.VMEM((ne, 2 * per, half), BF16), pltpu.SemaphoreType.DMA((ns,))],
-        out_hbm=(0,),
     )(keep, to_seq(out, 1))
     rows_back = to_all(send)
 
@@ -322,8 +311,9 @@
         y, dx = [], []
         for core in range(2):
             got = [sum(in_ref[s * ne + e].astype(F32) for s in range(core, ns, 2)) for e in range(ne)]
-            y.append(jnp.concatenate([v[:per] for v in got], axis=0))
-            dx.append(jnp.concatenate([v[per:] for v in got], axis=0))
+            both = jnp.concatenate(got, axis=0)
+            y.append(both[:, :half])
+            dx.append(both[:, half:])
         y, dx = (jnp.concatenate(v, axis=1).astype(BF16) for v in (y, dx))
         dxf = dx.astype(F32)
         inner = jnp.sum(dxf * a_ref[...], axis=1, keepdims=True)

time: 48.9 us -> 48.9 us (level)
  no operation moved by 1% of the time
where the time goes in v3:
time: 48.9 us; the launch traced here: 48.6 us
  blocking collectives  15.1 us (31%)
  Pallas kernels  13.4 us (27%)
  waiting for transfers between devices  10 us (20%)
  starting transfers between devices  8.13 us (17%)
  local copies, waits for them, and re-layouts  1.3 us (3%)
  between operations  0.72 us (1%)
    all_to_all x1, blocking collectives, to_all(): return lax.all_to_all(x, ('seq', 'exp'), 0, 0, tiled=True)  15.1 us
    pallas_call x11, Pallas kernels, run(): pl.pallas_call(body, out_shape=tuple((jax.ShapeDtypeStruct(s, d) for s, d...  13.4 us
    all_to_all x2, waiting for transfers between devices, to_all(): return lax.all_to_all(x, ('seq', 'exp'), 0, 0, tiled=True)  9.03 us
    all_to_all x2, starting transfers between devices, to_all(): return lax.all_to_all(x, ('seq', 'exp'), 0, 0, tiled=True)  5.89 us
    ppermute x3, starting transfers between devices, to_seq(): return lax.ppermute(x, 'seq', [(i, i ^ k) for i in range(ns)])  2.23 us
    unnamed x10, local copies, waits for them, and re-layouts  1.3 us
    ppermute x3, waiting for transfers between devices, to_seq(): return lax.ppermute(x, 'seq', [(i, i ^ k) for i in range(ns)])  0.99 us
  transfers between devices with their start and end apart: 5, of which 3 were waited for; matrix products, arithmetic and copies ran while one was open for 0% of the time, Pallas kernels for 14%

profile of v3, /device:TPU:0, one launch (start us, length us, event | category | flops | bytes accessed | tf_op | source)
XLA Modules:
  0.0 48.6 jit_solution(12555736934583251161)
XLA Ops:
  0.6 0.0 copy-start
  0.6 0.0 copy-start.4
  0.7 0.0 copy-start.1
  0.7 1.3 %copy-done = bf16[1,512,1280]{2,1,0:T(8,128)(2,1)S(1)} copy-done((bf16[1,512,1280]{2,1,0:T(8,128)(2,1)S(1)}, bf16[1,512,1280]{2,1,0:T(8,128)(2,1)}, u32[]{:S(2)}) %copy-start) | copy-done | bytes 1310744
  1.9 0.0 copy-done.4
  2.0 0.8 %shard_map.93 = (f32[16,1408]{1,0:T(8,128)S(1)}, bf16[16,512]{1,0:T(8,128)(2,1)S(1)}) custom-call(bf16[512,1280]{1,0:T(8,128)(2,1)S(1)} %bitcast.10, bf16[16,1280]{1,0:T(8,128)(2,1)S(1)} %bitcast.17, f32[8,128]{1,0:T(8,128)S(1)} %shard_map.92._), custom_call_target="tpu_custom_call" | custom-call | flops 41943040 | bytes 1310720 | tf_op jit(solution)/shard_map/pallas_call | solution.py:55
  2.7 0.0 copy-done.1
  2.7 0.3 shard_map.94
  3.0 0.5 collective-permute-start
  3.5 1.0 %collective-permute-done.r_ref = f32[16,2048]{1,0:T(8,128)S(1)} collective-permute-done((f32[16,2048]{1,0:T(8,128)S(1)}, f32[16,2048]{1,0:T(8,128)S(1)}, u32[]{:S(2)}, u32[]{:S(2)}) %collective-permute-start) | collective-permute-done | bytes 131104 | tf_op jit(solution)/shard_map/ppermute | solution.py:79
  4.5 0.0 copy-start.2
  4.5 0.0 copy-start.3
  4.5 0.2 shard_map.95
  4.7 15.1 %all_to_all.15.refs_1_ = bf16[32,2,1408]{2,1,0:T(2,128)(2,1)S(1)} all-to-all(bf16[32,2,1408]{2,1,0:T(2,128)(2,1)S(1)} %get-tuple-element.33), channel_id=1, replica_groups=mesh['seq'=4,'exp'=8] {'seq','exp'}, dimensions={0} | all-to-all | bytes 360448 | tf_op jit(solution)/shard_map/all_to_all | solution.py:82
  19.7 0.0 copy-done.2
  19.7 0.0 copy-done.3
  19.7 2.8 %shard_map.96 = (bf16[16,1280]{1,0:T(8,128)(2,1)S(1)}, bf16[16,1280]{1,0:T(8,128)(2,1)S(1)}, bf16[16,1280]{1,0:T(8,128)(2,1)S(1)}, bf16[16,1280]{1,0:T(8,128)(2,...) custom-call(bf16[1280,1280]{1,0:T(8,128)(2,1)S(1)} %bitcast.15, bf16[32,2,1408]{2,1,0:T(2,128)(2,1)S(1)} %all_to_all.15.refs_1_, ...), custom_call_target="tpu_custom_call" | custom-call | flops 209715200 | bytes 6553600 | tf_op jit(solution)/shard_map/pallas_call | solution.py:55
  22.6 0.3 collective-permute-start.2
  22.8 1.5 %collective-permute-start.1 = (f32[16,1408]{1,0:T(8,128)S(1)}, f32[16,1408]{1,0:T(8,128)S(1)}, u32[]{:S(2)}, u32[]{:S(2)}) collective-permute-start(f32[16,1408]{1,0:T(8,128)S(1)} %get-tuple-element.39.l_ref), channel_id=1, source_target_pairs={{0,16},{8,24},{16,0},{24,8},{1,17},{9,25},{17,1},{25,9},{2,18},{10... | collective-permute-start | bytes 270344 | tf_op jit(solution)/shard_map/ppermute | solution.py:79
  24.3 0.0 collective-permute-done.2.r_ref
  24.3 0.7 %shard_map.99 = bf16[32,2,1280]{2,1,0:T(2,128)(2,1)} custom-call(f32[16,1280]{1,0:T(8,128)S(1)} %get-tuple-element.42.l_ref, f32[16,1280]{1,0:T(8,128)S(1)} %collective-permute-done.2.r_ref), custom_call_target="tpu_custom_call" | custom-call | flops 40960 | bytes 163840 | tf_op jit(solution)/shard_map/pallas_call | solution.py:55
  25.0 2.9 %all-to-all-start.1 = ((bf16[32,2,1280]{2,1,0:T(2,128)(2,1)}), bf16[32,2,1280]{2,1,0:T(2,128)(2,1)S(1)}, u32[]{:S(2)}, u32[]{:S(2)}) async-start(bf16[32,2,1280]{2,1,0:T(2,128)(2,1)} %shard_map.99), calls=%async_computation.1 | async-start | bytes 327680 | tf_op jit(solution)/shard_map/all_to_all | solution.py:82
  28.0 3.2 %shard_map.97 = (bf16[1280,1280]{1,0:T(8,128)(2,1)}, bf16[1280,1280]{1,0:T(8,128)(2,1)}, f32[8,128]{1,0:T(8,128)S(1)}) custom-call(bf16[16,1280]{1,0:T(8,128)(2,1)S(1)} %get-tuple-element.34.refs_0_, bf16[16,1280]{1,0:T(8,128)(2,1)S(1)} %get-tuple-element.35.refs_1_, bf16[16,1280]{1,0:T(8,128)(2,1)S(1)} %get-tuple-element.36.refs_2_, ...), custom_call_target="tpu_custom_call" | custom-call | flops 68719476736 | bytes 6553600 | tf_op jit(solution)/shard_map/pallas_call | solution.py:55
  31.2 0.0 collective-permute-done.1.r_ref
  31.2 0.5 shard_map.98
  31.7 4.2 %all-to-all-done.1.in_ref = bf16[32,2,1280]{2,1,0:T(2,128)(2,1)S(1)} async-done(((bf16[32,2,1280]{2,1,0:T(2,128)(2,1)}), bf16[32,2,1280]{2,1,0:T(2,128)(2,1)S(1)}, u32[]{:S(2)}, u32[]{:S(2)}) %all-to-all-start.1) | async-done | bytes 163872 | tf_op jit(solution)/shard_map/all_to_all | solution.py:82
  35.9 1.8 %shard_map.100 = (bf16[16,512]{1,0:T(8,128)(2,1)S(1)}, bf16[16,1280]{1,0:T(8,128)(2,1)S(1)}, bf16[16,1280]{1,0:T(8,128)(2,1)S(1)}, bf16[32,8,80]{2,1,0:T(8,128)(2,1)}) custom-call(bf16[32,2,1280]{2,1,0:T(2,128)(2,1)S(1)} %all-to-all-done.1.in_ref, f32[16,1280]{1,0:T(8,128)S(1)} %get-tuple-element.44.a_ref, f32[16,512]{1,0:T(8,128)S(1)} %get-tuple-element.40.c_ref.refs_0_, ...), custom_call_target="tpu_custom_call" | custom-call | flops 62914560 | bytes 2621440 | tf_op jit(solution)/shard_map/pallas_call | solution.py:55
  37.6 3.0 %all-to-all-start.2 = ((bf16[32,8,80]{2,1,0:T(8,128)(2,1)}), bf16[32,8,80]{2,1,0:T(8,128)(2,1)S(1)}, u32[]{:S(2)}, u32[]{:S(2)}) async-start(bf16[32,8,80]{2,1,0:T(8,128)(2,1)} %get-tuple-element.50), calls=%async_computation.2 | async-start | bytes 131072 | tf_op jit(solution)/shard_map/all_to_all | solution.py:82
  40.6 2.4 %shard_map.101 = (bf16[512,1280]{1,0:T(8,128)(2,1)}, bf16[512,1280]{1,0:T(8,128)(2,1)}, f32[8,128]{1,0:T(8,128)}) custom-call(f32[16,512]{1,0:T(8,128)S(1)} %get-tuple-element.40.c_ref.refs_0_, f32[16,512]{1,0:T(8,128)S(1)} %get-tuple-element.41.d_ref.refs_1_, bf16[16,512]{1,0:T(8,128)(2,1)S(1)} %get-tuple-element.45.refs_2_, ...), custom_call_target="tpu_custom_call" | custom-call | flops 68719476736 | bytes 2621440 | tf_op jit(solution)/shard_map/pallas_call | solution.py:55
  43.1 4.8 %all-to-all-done.2.in_ref = bf16[32,8,80]{2,1,0:T(8,128)(2,1)S(1)} async-done(((bf16[32,8,80]{2,1,0:T(8,128)(2,1)}), bf16[32,8,80]{2,1,0:T(8,128)(2,1)S(1)}, u32[]{:S(2)}, u32[]{:S(2)}) %all-to-all-start.2) | async-done | bytes 40992 | tf_op jit(solution)/shard_map/all_to_all | solution.py:82
  47.9 0.7 %shard_map.102 = f32[16,40]{1,0:T(8,128)} custom-call(bf16[32,8,80]{2,1,0:T(8,128)(2,1)S(1)} %all-to-all-done.2.in_ref), custom_call_target="tpu_custom_call" | custom-call | flops 20480 | bytes 81920 | tf_op jit(solution)/shard_map/pallas_call | solution.py:55
  (1 shorter events, 0.0 us)
Async XLA Ops:
  0.6 1.3 %copy-start = (bf16[1,512,1280]{2,1,0:T(8,128)(2,1)S(1)}, bf16[1,512,1280]{2,1,0:T(8,128)(2,1)}, u32[]{:S(2)}) copy-start(bf16[1,512,1280]{2,1,0:T(8,128)(2,1)} %param.5) | copy-start | bytes 3932164
  0.6 1.3 %copy-start.4 = (bf16[1280,16]{0,1:T(8,128)(2,1)S(1)}, bf16[1280,16]{0,1:T(8,128)(2,1)}, u32[]{:S(2)}) copy-start(bf16[1280,16]{0,1:T(8,128)(2,1)} %param.6) | copy-start | bytes 122884
  0.7 2.1 %copy-start.1 = (bf16[1,512,1280]{2,1,0:T(8,128)(2,1)S(1)}, bf16[1,512,1280]{2,1,0:T(8,128)(2,1)}, u32[]{:S(2)}) copy-start(bf16[1,512,1280]{2,1,0:T(8,128)(2,1)} %param.9) | copy-start | bytes 3932164
  3.0 1.5 %collective-permute-start = (f32[16,2048]{1,0:T(8,128)S(1)}, f32[16,2048]{1,0:T(8,128)S(1)}, u32[]{:S(2)}, u32[]{:S(2)}) collective-permute-start(f32[16,2048]{1,0:T(8,128)S(1)} %get-tuple-element.31.l_ref), channel_id=1, source_target_pairs={{0,8},{8,0},{16,24},{24,16},{1,9},{9,1},{17,25},{25,17},{2,10},{10... | collective-permute-start | bytes 393224 | tf_op jit(solution)/shard_map/ppermute | solution.py:79
  4.5 15.2 %copy-start.2 = (bf16[1,1280,1280]{2,1,0:T(8,128)(2,1)S(1)}, bf16[1,1280,1280]{2,1,0:T(8,128)(2,1)}, u32[]{:S(2)}) copy-start(bf16[1,1280,1280]{2,1,0:T(8,128)(2,1)} %param.8) | copy-start | bytes 9830404
  4.5 15.2 %copy-start.3 = (bf16[1,1280,1280]{2,1,0:T(8,128)(2,1)S(1)}, bf16[1,1280,1280]{2,1,0:T(8,128)(2,1)}, u32[]{:S(2)}) copy-start(bf16[1,1280,1280]{2,1,0:T(8,128)(2,1)} %param.7) | copy-start | bytes 9830404
  22.6 1.8 %collective-permute-start.2 = (f32[16,1280]{1,0:T(8,128)S(1)}, f32[16,1280]{1,0:T(8,128)S(1)}, u32[]{:S(2)}, u32[]{:S(2)}) collective-permute-start(f32[16,1280]{1,0:T(8,128)S(1)} %get-tuple-element.43), channel_id=1, source_target_pairs={{0,8},{8,0},{16,24},{24,16},{1,9},{9,1},{17,25},{25,17},{2,10},{10... | collective-permute-start | bytes 245768 | tf_op jit(solution)/shard_map/ppermute | solution.py:79
  22.8 8.3 %collective-permute-start.1 = (f32[16,1408]{1,0:T(8,128)S(1)}, f32[16,1408]{1,0:T(8,128)S(1)}, u32[]{:S(2)}, u32[]{:S(2)}) collective-permute-start(f32[16,1408]{1,0:T(8,128)S(1)} %get-tuple-element.39.l_ref), channel_id=1, source_target_pairs={{0,16},{8,24},{16,0},{24,8},{1,17},{9,25},{17,1},{25,9},{2,18},{10... | collective-permute-start | bytes 270344 | tf_op jit(solution)/shard_map/ppermute | solution.py:79
  25.0 10.8 %all-to-all-start.1 = ((bf16[32,2,1280]{2,1,0:T(2,128)(2,1)}), bf16[32,2,1280]{2,1,0:T(2,128)(2,1)S(1)}, u32[]{:S(2)}, u32[]{:S(2)}) async-start(bf16[32,2,1280]{2,1,0:T(2,128)(2,1)} %shard_map.99), calls=%async_computation.1 | async-start | bytes 327680 | tf_op jit(solution)/shard_map/all_to_all | solution.py:82
  37.6 10.3 %all-to-all-start.2 = ((bf16[32,8,80]{2,1,0:T(8,128)(2,1)}), bf16[32,8,80]{2,1,0:T(8,128)(2,1)S(1)}, u32[]{:S(2)}, u32[]{:S(2)}) async-start(bf16[32,8,80]{2,1,0:T(8,128)(2,1)} %get-tuple-element.50), calls=%async_computation.2 | async-start | bytes 131072 | tf_op jit(solution)/shard_map/all_to_all | solution.py:82

commit v4 on v3

--- a/solution.py
+++ b/solution.py
@@ -74,6 +74,7 @@
     half = width // 2
     wide = width + LANES
     cut = width // (ns * ne)
+    tile = pl.cdiv(2 * cut + 1, LANES) * LANES
 
     def to_seq(x, k):
         return lax.ppermute(x, "seq", [(i, i ^ k) for i in range(ns)])
@@ -328,9 +329,11 @@
         l_ref[...] = d_logit
         y_ref[...] = y
         dx_ref[...] = dx
+        fill = [jnp.zeros((slots // 2, tile - 2 * cut), F32)]
         for k in range(ns * ne):
             piece = d_route[:, k * cut : (k + 1) * cut]
-            out[k] = jnp.concatenate([piece[: slots // 2], piece[slots // 2 :]], axis=1).astype(BF16)
+            parts = [piece[: slots // 2], piece[slots // 2 :]] + fill
+            out[k] = jnp.concatenate(parts, axis=1).astype(BF16)
 
     d_logit, y, dx, send = call(
         logit_kernel,
@@ -338,7 +341,7 @@
             ((slots, length), BF16),
             ((slots, width), BF16),
             ((slots, width), BF16),
-            ((ns * ne, slots // 2, 2 * cut), BF16),
+            ((ns * ne, slots // 2, tile), BF16),
         ],
         24,
         6 * slots * length * width,
@@ -357,7 +360,7 @@
 
     def sum_kernel(in_ref, out_ref):
         full = jnp.sum(in_ref[...].astype(F32), axis=0)
-        out_ref[...] = jnp.concatenate([full[:, :cut], full[:, cut:]], axis=0)
+        out_ref[...] = jnp.concatenate([full[:, :cut], full[:, cut : 2 * cut]], axis=0)
 
     (d_router,) = call(
         sum_kernel, [((slots, cut), F32)], 8, slots * width, slots * width * 4

time: 48.9 us -> 48.9 us (level)
  no operation moved by 1% of the time
where the time goes in v4:
time: 48.9 us; the launch traced here: 48.6 us
  blocking collectives  15.1 us (31%)
  Pallas kernels  13.4 us (27%)
  waiting for transfers between devices  10 us (20%)
  starting transfers between devices  8.13 us (17%)
  local copies, waits for them, and re-layouts  1.3 us (3%)
  between operations  0.72 us (1%)
    all_to_all x1, blocking collectives, to_all(): return lax.all_to_all(x, ('seq', 'exp'), 0, 0, tiled=True)  15.1 us
    pallas_call x11, Pallas kernels, run(): pl.pallas_call(body, out_shape=tuple((jax.ShapeDtypeStruct(s, d) for s, d...  13.4 us
    all_to_all x2, waiting for transfers between devices, to_all(): return lax.all_to_all(x, ('seq', 'exp'), 0, 0, tiled=True)  9.03 us
    all_to_all x2, starting transfers between devices, to_all(): return lax.all_to_all(x, ('seq', 'exp'), 0, 0, tiled=True)  5.89 us
    ppermute x3, starting transfers between devices, to_seq(): return lax.ppermute(x, 'seq', [(i, i ^ k) for i in range(ns)])  2.23 us
    unnamed x10, local copies, waits for them, and re-layouts  1.3 us
    ppermute x3, waiting for transfers between devices, to_seq(): return lax.ppermute(x, 'seq', [(i, i ^ k) for i in range(ns)])  0.99 us
  transfers between devices with their start and end apart: 5, of which 3 were waited for; matrix products, arithmetic and copies ran while one was open for 0% of the time, Pallas kernels for 14%

profile of v4, /device:TPU:0, one launch (start us, length us, event | category | flops | bytes accessed | tf_op | source)
XLA Modules:
  0.0 48.6 jit_solution(5833288380884597517)
XLA Ops:
  0.6 0.0 copy-start
  0.6 0.0 copy-start.4
  0.7 0.0 copy-start.1
  0.7 1.3 %copy-done = bf16[1,512,1280]{2,1,0:T(8,128)(2,1)S(1)} copy-done((bf16[1,512,1280]{2,1,0:T(8,128)(2,1)S(1)}, bf16[1,512,1280]{2,1,0:T(8,128)(2,1)}, u32[]{:S(2)}) %copy-start) | copy-done | bytes 1310744
  1.9 0.0 copy-done.4
  2.0 0.8 %shard_map.93 = (f32[16,1408]{1,0:T(8,128)S(1)}, bf16[16,512]{1,0:T(8,128)(2,1)S(1)}) custom-call(bf16[512,1280]{1,0:T(8,128)(2,1)S(1)} %bitcast.10, bf16[16,1280]{1,0:T(8,128)(2,1)S(1)} %bitcast.17, f32[8,128]{1,0:T(8,128)S(1)} %shard_map.92._), custom_call_target="tpu_custom_call" | custom-call | flops 41943040 | bytes 1310720 | tf_op jit(solution)/shard_map/pallas_call | solution.py:55
  2.7 0.0 copy-done.1
  2.7 0.3 shard_map.94
  3.0 0.5 collective-permute-start
  3.5 1.0 %collective-permute-done.r_ref = f32[16,2048]{1,0:T(8,128)S(1)} collective-permute-done((f32[16,2048]{1,0:T(8,128)S(1)}, f32[16,2048]{1,0:T(8,128)S(1)}, u32[]{:S(2)}, u32[]{:S(2)}) %collective-permute-start) | collective-permute-done | bytes 131104 | tf_op jit(solution)/shard_map/ppermute | solution.py:80
  4.5 0.0 copy-start.2
  4.5 0.0 copy-start.3
  4.5 0.2 shard_map.95
  4.7 15.1 %all_to_all.15.refs_1_ = bf16[32,2,1408]{2,1,0:T(2,128)(2,1)S(1)} all-to-all(bf16[32,2,1408]{2,1,0:T(2,128)(2,1)S(1)} %get-tuple-element.33), channel_id=1, replica_groups=mesh['seq'=4,'exp'=8] {'seq','exp'}, dimensions={0} | all-to-all | bytes 360448 | tf_op jit(solution)/shard_map/all_to_all | solution.py:83
  19.7 0.0 copy-done.2
  19.7 0.0 copy-done.3
  19.7 2.8 %shard_map.96 = (bf16[16,1280]{1,0:T(8,128)(2,1)S(1)}, bf16[16,1280]{1,0:T(8,128)(2,1)S(1)}, bf16[16,1280]{1,0:T(8,128)(2,1)S(1)}, bf16[16,1280]{1,0:T(8,128)(2,...) custom-call(bf16[1280,1280]{1,0:T(8,128)(2,1)S(1)} %bitcast.15, bf16[32,2,1408]{2,1,0:T(2,128)(2,1)S(1)} %all_to_all.15.refs_1_, ...), custom_call_target="tpu_custom_call" | custom-call | flops 209715200 | bytes 6553600 | tf_op jit(solution)/shard_map/pallas_call | solution.py:55
  22.6 0.3 collective-permute-start.2
  22.8 1.5 %collective-permute-start.1 = (f32[16,1408]{1,0:T(8,128)S(1)}, f32[16,1408]{1,0:T(8,128)S(1)}, u32[]{:S(2)}, u32[]{:S(2)}) collective-permute-start(f32[16,1408]{1,0:T(8,128)S(1)} %get-tuple-element.39.l_ref), channel_id=1, source_target_pairs={{0,16},{8,24},{16,0},{24,8},{1,17},{9,25},{17,1},{25,9},{2,18},{10... | collective-permute-start | bytes 270344 | tf_op jit(solution)/shard_map/ppermute | solution.py:80
  24.3 0.0 collective-permute-done.2.r_ref
  24.3 0.7 %shard_map.99 = bf16[32,2,1280]{2,1,0:T(2,128)(2,1)} custom-call(f32[16,1280]{1,0:T(8,128)S(1)} %get-tuple-element.42.l_ref, f32[16,1280]{1,0:T(8,128)S(1)} %collective-permute-done.2.r_ref), custom_call_target="tpu_custom_call" | custom-call | flops 40960 | bytes 163840 | tf_op jit(solution)/shard_map/pallas_call | solution.py:55
  25.0 2.9 %all-to-all-start.1 = ((bf16[32,2,1280]{2,1,0:T(2,128)(2,1)}), bf16[32,2,1280]{2,1,0:T(2,128)(2,1)S(1)}, u32[]{:S(2)}, u32[]{:S(2)}) async-start(bf16[32,2,1280]{2,1,0:T(2,128)(2,1)} %shard_map.99), calls=%async_computation.1 | async-start | bytes 327680 | tf_op jit(solution)/shard_map/all_to_all | solution.py:83
  28.0 3.2 %shard_map.97 = (bf16[1280,1280]{1,0:T(8,128)(2,1)}, bf16[1280,1280]{1,0:T(8,128)(2,1)}, f32[8,128]{1,0:T(8,128)S(1)}) custom-call(bf16[16,1280]{1,0:T(8,128)(2,1)S(1)} %get-tuple-element.34.refs_0_, bf16[16,1280]{1,0:T(8,128)(2,1)S(1)} %get-tuple-element.35.refs_1_, bf16[16,1280]{1,0:T(8,128)(2,1)S(1)} %get-tuple-element.36.refs_2_, ...), custom_call_target="tpu_custom_call" | custom-call | flops 68719476736 | bytes 6553600 | tf_op jit(solution)/shard_map/pallas_call | solution.py:55
  31.2 0.0 collective-permute-done.1.r_ref
  31.2 0.5 shard_map.98
  31.7 4.2 %all-to-all-done.1.in_ref = bf16[32,2,1280]{2,1,0:T(2,128)(2,1)S(1)} async-done(((bf16[32,2,1280]{2,1,0:T(2,128)(2,1)}), bf16[32,2,1280]{2,1,0:T(2,128)(2,1)S(1)}, u32[]{:S(2)}, u32[]{:S(2)}) %all-to-all-start.1) | async-done | bytes 163872 | tf_op jit(solution)/shard_map/all_to_all | solution.py:83
  35.9 1.8 %shard_map.100 = (bf16[16,512]{1,0:T(8,128)(2,1)S(1)}, bf16[16,1280]{1,0:T(8,128)(2,1)S(1)}, bf16[16,1280]{1,0:T(8,128)(2,1)S(1)}, bf16[32,8,128]{2,1,0:T(8,128)(2,1)}) custom-call(bf16[32,2,1280]{2,1,0:T(2,128)(2,1)S(1)} %all-to-all-done.1.in_ref, f32[16,1280]{1,0:T(8,128)S(1)} %get-tuple-element.44.a_ref, f32[16,512]{1,0:T(8,128)S(1)} %get-tuple-element.40.c_ref.refs_0_, ...), custom_call_target="tpu_custom_call" | custom-call | flops 62914560 | bytes 2621440 | tf_op jit(solution)/shard_map/pallas_call | solution.py:55
  37.6 3.0 %all-to-all-start.2 = ((bf16[32,8,128]{2,1,0:T(8,128)(2,1)}), bf16[32,8,128]{2,1,0:T(8,128)(2,1)S(1)}, u32[]{:S(2)}, u32[]{:S(2)}) async-start(bf16[32,8,128]{2,1,0:T(8,128)(2,1)} %get-tuple-element.50), calls=%async_computation.2 | async-start | bytes 131072 | tf_op jit(solution)/shard_map/all_to_all | solution.py:83
  40.6 2.4 %shard_map.101 = (bf16[512,1280]{1,0:T(8,128)(2,1)}, bf16[512,1280]{1,0:T(8,128)(2,1)}, f32[8,128]{1,0:T(8,128)}) custom-call(f32[16,512]{1,0:T(8,128)S(1)} %get-tuple-element.40.c_ref.refs_0_, f32[16,512]{1,0:T(8,128)S(1)} %get-tuple-element.41.d_ref.refs_1_, bf16[16,512]{1,0:T(8,128)(2,1)S(1)} %get-tuple-element.45.refs_2_, ...), custom_call_target="tpu_custom_call" | custom-call | flops 68719476736 | bytes 2621440 | tf_op jit(solution)/shard_map/pallas_call | solution.py:55
  43.1 4.8 %all-to-all-done.2.in_ref = bf16[32,8,128]{2,1,0:T(8,128)(2,1)S(1)} async-done(((bf16[32,8,128]{2,1,0:T(8,128)(2,1)}), bf16[32,8,128]{2,1,0:T(8,128)(2,1)S(1)}, u32[]{:S(2)}, u32[]{:S(2)}) %all-to-all-start.2) | async-done | bytes 65568 | tf_op jit(solution)/shard_map/all_to_all | solution.py:83
  47.9 0.7 %shard_map.102 = f32[16,40]{1,0:T(8,128)} custom-call(bf16[32,8,128]{2,1,0:T(8,128)(2,1)S(1)} %all-to-all-done.2.in_ref), custom_call_target="tpu_custom_call" | custom-call | flops 20480 | bytes 81920 | tf_op jit(solution)/shard_map/pallas_call | solution.py:55
  (1 shorter events, 0.0 us)
Async XLA Ops:
  0.6 1.3 %copy-start = (bf16[1,512,1280]{2,1,0:T(8,128)(2,1)S(1)}, bf16[1,512,1280]{2,1,0:T(8,128)(2,1)}, u32[]{:S(2)}) copy-start(bf16[1,512,1280]{2,1,0:T(8,128)(2,1)} %param.5) | copy-start | bytes 3932164
  0.6 1.3 %copy-start.4 = (bf16[1280,16]{0,1:T(8,128)(2,1)S(1)}, bf16[1280,16]{0,1:T(8,128)(2,1)}, u32[]{:S(2)}) copy-start(bf16[1280,16]{0,1:T(8,128)(2,1)} %param.6) | copy-start | bytes 122884
  0.7 2.1 %copy-start.1 = (bf16[1,512,1280]{2,1,0:T(8,128)(2,1)S(1)}, bf16[1,512,1280]{2,1,0:T(8,128)(2,1)}, u32[]{:S(2)}) copy-start(bf16[1,512,1280]{2,1,0:T(8,128)(2,1)} %param.9) | copy-start | bytes 3932164
  3.0 1.5 %collective-permute-start = (f32[16,2048]{1,0:T(8,128)S(1)}, f32[16,2048]{1,0:T(8,128)S(1)}, u32[]{:S(2)}, u32[]{:S(2)}) collective-permute-start(f32[16,2048]{1,0:T(8,128)S(1)} %get-tuple-element.31.l_ref), channel_id=1, source_target_pairs={{0,8},{8,0},{16,24},{24,16},{1,9},{9,1},{17,25},{25,17},{2,10},{10... | collective-permute-start | bytes 393224 | tf_op jit(solution)/shard_map/ppermute | solution.py:80
  4.5 15.2 %copy-start.2 = (bf16[1,1280,1280]{2,1,0:T(8,128)(2,1)S(1)}, bf16[1,1280,1280]{2,1,0:T(8,128)(2,1)}, u32[]{:S(2)}) copy-start(bf16[1,1280,1280]{2,1,0:T(8,128)(2,1)} %param.8) | copy-start | bytes 9830404
  4.5 15.2 %copy-start.3 = (bf16[1,1280,1280]{2,1,0:T(8,128)(2,1)S(1)}, bf16[1,1280,1280]{2,1,0:T(8,128)(2,1)}, u32[]{:S(2)}) copy-start(bf16[1,1280,1280]{2,1,0:T(8,128)(2,1)} %param.7) | copy-start | bytes 9830404
  22.6 1.8 %collective-permute-start.2 = (f32[16,1280]{1,0:T(8,128)S(1)}, f32[16,1280]{1,0:T(8,128)S(1)}, u32[]{:S(2)}, u32[]{:S(2)}) collective-permute-start(f32[16,1280]{1,0:T(8,128)S(1)} %get-tuple-element.43), channel_id=1, source_target_pairs={{0,8},{8,0},{16,24},{24,16},{1,9},{9,1},{17,25},{25,17},{2,10},{10... | collective-permute-start | bytes 245768 | tf_op jit(solution)/shard_map/ppermute | solution.py:80
  22.8 8.3 %collective-permute-start.1 = (f32[16,1408]{1,0:T(8,128)S(1)}, f32[16,1408]{1,0:T(8,128)S(1)}, u32[]{:S(2)}, u32[]{:S(2)}) collective-permute-start(f32[16,1408]{1,0:T(8,128)S(1)} %get-tuple-element.39.l_ref), channel_id=1, source_target_pairs={{0,16},{8,24},{16,0},{24,8},{1,17},{9,25},{17,1},{25,9},{2,18},{10... | collective-permute-start | bytes 270344 | tf_op jit(solution)/shard_map/ppermute | solution.py:80
  25.0 10.8 %all-to-all-start.1 = ((bf16[32,2,1280]{2,1,0:T(2,128)(2,1)}), bf16[32,2,1280]{2,1,0:T(2,128)(2,1)S(1)}, u32[]{:S(2)}, u32[]{:S(2)}) async-start(bf16[32,2,1280]{2,1,0:T(2,128)(2,1)} %shard_map.99), calls=%async_computation.1 | async-start | bytes 327680 | tf_op jit(solution)/shard_map/all_to_all | solution.py:83
  37.6 10.3 %all-to-all-start.2 = ((bf16[32,8,128]{2,1,0:T(8,128)(2,1)}), bf16[32,8,128]{2,1,0:T(8,128)(2,1)S(1)}, u32[]{:S(2)}, u32[]{:S(2)}) async-start(bf16[32,8,128]{2,1,0:T(8,128)(2,1)} %get-tuple-element.50), calls=%async_computation.2 | async-start | bytes 131072 | tf_op jit(solution)/shard_map/all_to_all | solution.py:83

commit v5 on v3

--- a/solution.py
+++ b/solution.py
@@ -99,11 +99,11 @@
         top = jnp.max(logits, axis=1, keepdims=True)
         p = jnp.exp(logits - top)
         p_b = p.astype(BF16)
+        part_ref[:, :width] = dot(p_b, x, 1, 0)
         total = jnp.sum(p, axis=1, keepdims=True)
         total_b = jnp.sum(p_b.astype(F32), axis=1, keepdims=True)
         e = jnp.exp(logits - jnp.max(logits, axis=0, keepdims=True))
         combine_ref[...] = (e / jnp.sum(e, axis=0, keepdims=True)).astype(BF16)
-        part_ref[:, :width] = dot(p_b, x, 1, 0)
         part_ref[:, width:] = stat_tile(top, total, total_b)
 
     part, combine_b = call(
@@ -169,6 +169,16 @@
     def expert_kernel(*refs):
         w2_ref, in_ref, w1_ref, x_ref, dy_ref, act_ref, dh_ref, out_ref, keep_ref, *scratch = refs
         (half_ref,) = scratch
+        dys = []
+        for core in range(2):
+            cut_rows = [
+                sum(in_ref[s * ne + c, :, half:width].astype(F32) for s in range(core, ns, 2))
+                for c in range(ne)
+            ]
+            dys.append(jnp.concatenate(cut_rows, axis=0))
+        dy = jnp.concatenate(dys, axis=1).astype(BF16)
+        w2v = w2_ref[...]
+        d_act = dot(dy, w2v, 1, 1)
         tops, totals = [], []
         for s in range(0, ns, 2):
             tile = jnp.concatenate(
@@ -180,24 +190,21 @@
         scale = [jnp.exp(m - top) for m in tops]
         total = sum(w * v for w, v in zip(scale, totals))
         scale = [w / total for w in scale]
-        xs, dys = [[], []], [[], []]
+        xs = []
         for core in range(2):
+            cut_rows = []
             for c in range(ne):
                 at = slice(c * per, (c + 1) * per)
-                x, dy = 0.0, 0.0
-                for w, s in zip(scale, range(core, ns, 2)):
-                    x += w[at] * in_ref[s * ne + c, :, :half].astype(F32)
-                    dy += in_ref[s * ne + c, :, half:width].astype(F32)
-                xs[core].append(x)
-                dys[core].append(dy)
-        x, dy = (
-            jnp.concatenate([jnp.concatenate(v, axis=0) for v in side], axis=1).astype(BF16)
-            for side in (xs, dys)
-        )
+                cut_rows.append(
+                    sum(
+                        w[at] * in_ref[s * ne + c, :, :half].astype(F32)
+                        for w, s in zip(scale, range(core, ns, 2))
+                    )
+                )
+            xs.append(jnp.concatenate(cut_rows, axis=0))
+        x = jnp.concatenate(xs, axis=1).astype(BF16)
         x_ref[...] = x
         dy_ref[...] = dy
-        w2v = w2_ref[...]
-        d_act = dot(dy, w2v, 1, 1)
         act, slope = gelu_parts(dot(x, w1_ref[...], 1, 0))
         act = act.astype(BF16)
         act_ref[...] = act
@@ -308,21 +315,27 @@
     )(written, part, to_seq(part, 1 << (bits - 1)), router.T, feats)
 
     def logit_kernel(in_ref, a_ref, c_ref, d_ref, x_ref, g_ref, l_ref, y_ref, dx_ref, out):
-        y, dx = [], []
-        for core in range(2):
-            got = [sum(in_ref[s * ne + e].astype(F32) for s in range(core, ns, 2)) for e in range(ne)]
-            both = jnp.concatenate(got, axis=0)
-            y.append(both[:, :half])
-            dx.append(both[:, half:])
-        y, dx = (jnp.concatenate(v, axis=1).astype(BF16) for v in (y, dx))
+        def rows(at):
+            sides = []
+            for core in range(2):
+                got = [
+                    sum(in_ref[s * ne + e, :, at].astype(F32) for s in range(core, ns, 2))
+                    for e in range(ne)
+                ]
+                sides.append(jnp.concatenate(got, axis=0))
+            return jnp.concatenate(sides, axis=1).astype(BF16)
+
+        y = rows(slice(0, half))
+        d_combine = dot(y, g_ref[...], 1, 1)
+        dx = rows(slice(half, width))
+        x = x_ref[...]
+        d_dispatch = dot(dx, x, 1, 1)
         dxf = dx.astype(F32)
         inner = jnp.sum(dxf * a_ref[...], axis=1, keepdims=True)
-        x = x_ref[...]
         combine = c_ref[...]
         dispatch = d_ref[...]
-        d_combine = dot(y, g_ref[...], 1, 1)
         d_c = combine * (d_combine - jnp.sum(combine * d_combine, axis=0, keepdims=True))
-        d_d = dispatch * (dot(dx, x, 1, 1) - inner)
+        d_d = dispatch * (d_dispatch - inner)
         d_logit = (d_c + d_d).astype(BF16)
         d_route = dot(d_logit, x, 1, 0)
         l_ref[...] = d_logit

time: 48.9 us -> 48.9 us (level)
  no operation moved by 1% of the time
where the time goes in v5:
time: 48.9 us; the launch traced here: 48.6 us
  blocking collectives  15.1 us (31%)
  Pallas kernels  13.4 us (27%)
  waiting for transfers between devices  10 us (20%)
  starting transfers between devices  8.13 us (17%)
  local copies, waits for them, and re-layouts  1.3 us (3%)
  between operations  0.72 us (1%)
    all_to_all x1, blocking collectives, to_all(): return lax.all_to_all(x, ('seq', 'exp'), 0, 0, tiled=True)  15.1 us
    pallas_call x11, Pallas kernels, run(): pl.pallas_call(body, out_shape=tuple((jax.ShapeDtypeStruct(s, d) for s, d...  13.4 us
    all_to_all x2, waiting for transfers between devices, to_all(): return lax.all_to_all(x, ('seq', 'exp'), 0, 0, tiled=True)  9.04 us
    all_to_all x2, starting transfers between devices, to_all(): return lax.all_to_all(x, ('seq', 'exp'), 0, 0, tiled=True)  5.89 us
    ppermute x3, starting transfers between devices, to_seq(): return lax.ppermute(x, 'seq', [(i, i ^ k) for i in range(ns)])  2.23 us
    unnamed x10, local copies, waits for them, and re-layouts  1.3 us
    ppermute x3, waiting for transfers between devices, to_seq(): return lax.ppermute(x, 'seq', [(i, i ^ k) for i in range(ns)])  0.99 us
  transfers between devices with their start and end apart: 5, of which 3 were waited for; matrix products, arithmetic and copies ran while one was open for 0% of the time, Pallas kernels for 14%

profile of v5, /device:TPU:0, one launch (start us, length us, event | category | flops | bytes accessed | tf_op | source)
XLA Modules:
  0.0 48.6 jit_solution(11117191577508646191)
XLA Ops:
  0.6 0.0 copy-start
  0.6 0.0 copy-start.4
  0.7 0.0 copy-start.1
  0.7 1.3 %copy-done = bf16[1,512,1280]{2,1,0:T(8,128)(2,1)S(1)} copy-done((bf16[1,512,1280]{2,1,0:T(8,128)(2,1)S(1)}, bf16[1,512,1280]{2,1,0:T(8,128)(2,1)}, u32[]{:S(2)}) %copy-start) | copy-done | bytes 1310744
  1.9 0.0 copy-done.4
  2.0 0.8 %shard_map.93 = (f32[16,1408]{1,0:T(8,128)S(1)}, bf16[16,512]{1,0:T(8,128)(2,1)S(1)}) custom-call(bf16[512,1280]{1,0:T(8,128)(2,1)S(1)} %bitcast.10, bf16[16,1280]{1,0:T(8,128)(2,1)S(1)} %bitcast.17, f32[8,128]{1,0:T(8,128)S(1)} %shard_map.92._), custom_call_target="tpu_custom_call" | custom-call | flops 41943040 | bytes 1310720 | tf_op jit(solution)/shard_map/pallas_call | solution.py:55
  2.7 0.0 copy-done.1
  2.7 0.3 shard_map.94
  3.0 0.5 collective-permute-start
  3.5 1.0 %collective-permute-done.r_ref = f32[16,2048]{1,0:T(8,128)S(1)} collective-permute-done((f32[16,2048]{1,0:T(8,128)S(1)}, f32[16,2048]{1,0:T(8,128)S(1)}, u32[]{:S(2)}, u32[]{:S(2)}) %collective-permute-start) | collective-permute-done | bytes 131104 | tf_op jit(solution)/shard_map/ppermute | solution.py:79
  4.5 0.0 copy-start.2
  4.5 0.0 copy-start.3
  4.5 0.2 shard_map.95
  4.7 15.1 %all_to_all.15.refs_1_ = bf16[32,2,1408]{2,1,0:T(2,128)(2,1)S(1)} all-to-all(bf16[32,2,1408]{2,1,0:T(2,128)(2,1)S(1)} %get-tuple-element.33), channel_id=1, replica_groups=mesh['seq'=4,'exp'=8] {'seq','exp'}, dimensions={0} | all-to-all | bytes 360448 | tf_op jit(solution)/shard_map/all_to_all | solution.py:82
  19.7 0.0 copy-done.2
  19.7 0.0 copy-done.3
  19.7 2.8 %shard_map.96 = (bf16[16,1280]{1,0:T(8,128)(2,1)S(1)}, bf16[16,1280]{1,0:T(8,128)(2,1)S(1)}, bf16[16,1280]{1,0:T(8,128)(2,1)S(1)}, bf16[16,1280]{1,0:T(8,128)(2,...) custom-call(bf16[1280,1280]{1,0:T(8,128)(2,1)S(1)} %bitcast.15, bf16[32,2,1408]{2,1,0:T(2,128)(2,1)S(1)} %all_to_all.15.refs_1_, ...), custom_call_target="tpu_custom_call" | custom-call | flops 209715200 | bytes 6553600 | tf_op jit(solution)/shard_map/pallas_call | solution.py:55
  22.6 0.3 collective-permute-start.2
  22.8 1.5 %collective-permute-start.1 = (f32[16,1408]{1,0:T(8,128)S(1)}, f32[16,1408]{1,0:T(8,128)S(1)}, u32[]{:S(2)}, u32[]{:S(2)}) collective-permute-start(f32[16,1408]{1,0:T(8,128)S(1)} %get-tuple-element.39.l_ref), channel_id=1, source_target_pairs={{0,16},{8,24},{16,0},{24,8},{1,17},{9,25},{17,1},{25,9},{2,18},{10... | collective-permute-start | bytes 270344 | tf_op jit(solution)/shard_map/ppermute | solution.py:79
  24.3 0.0 collective-permute-done.2.r_ref
  24.3 0.7 %shard_map.99 = bf16[32,2,1280]{2,1,0:T(2,128)(2,1)} custom-call(f32[16,1280]{1,0:T(8,128)S(1)} %get-tuple-element.42.l_ref, f32[16,1280]{1,0:T(8,128)S(1)} %collective-permute-done.2.r_ref), custom_call_target="tpu_custom_call" | custom-call | flops 40960 | bytes 163840 | tf_op jit(solution)/shard_map/pallas_call | solution.py:55
  25.0 2.9 %all-to-all-start.1 = ((bf16[32,2,1280]{2,1,0:T(2,128)(2,1)}), bf16[32,2,1280]{2,1,0:T(2,128)(2,1)S(1)}, u32[]{:S(2)}, u32[]{:S(2)}) async-start(bf16[32,2,1280]{2,1,0:T(2,128)(2,1)} %shard_map.99), calls=%async_computation.1 | async-start | bytes 327680 | tf_op jit(solution)/shard_map/all_to_all | solution.py:82
  28.0 3.2 %shard_map.97 = (bf16[1280,1280]{1,0:T(8,128)(2,1)}, bf16[1280,1280]{1,0:T(8,128)(2,1)}, f32[8,128]{1,0:T(8,128)S(1)}) custom-call(bf16[16,1280]{1,0:T(8,128)(2,1)S(1)} %get-tuple-element.34.refs_0_, bf16[16,1280]{1,0:T(8,128)(2,1)S(1)} %get-tuple-element.35.refs_1_, bf16[16,1280]{1,0:T(8,128)(2,1)S(1)} %get-tuple-element.36.refs_2_, ...), custom_call_target="tpu_custom_call" | custom-call | flops 68719476736 | bytes 6553600 | tf_op jit(solution)/shard_map/pallas_call | solution.py:55
  31.2 0.0 collective-permute-done.1.r_ref
  31.2 0.5 shard_map.98
  31.7 4.2 %all-to-all-done.1.in_ref = bf16[32,2,1280]{2,1,0:T(2,128)(2,1)S(1)} async-done(((bf16[32,2,1280]{2,1,0:T(2,128)(2,1)}), bf16[32,2,1280]{2,1,0:T(2,128)(2,1)S(1)}, u32[]{:S(2)}, u32[]{:S(2)}) %all-to-all-start.1) | async-done | bytes 163872 | tf_op jit(solution)/shard_map/all_to_all | solution.py:82
  35.9 1.8 %shard_map.100 = (bf16[16,512]{1,0:T(8,128)(2,1)S(1)}, bf16[16,1280]{1,0:T(8,128)(2,1)S(1)}, bf16[16,1280]{1,0:T(8,128)(2,1)S(1)}, bf16[32,8,80]{2,1,0:T(8,128)(2,1)}) custom-call(bf16[32,2,1280]{2,1,0:T(2,128)(2,1)S(1)} %all-to-all-done.1.in_ref, f32[16,1280]{1,0:T(8,128)S(1)} %get-tuple-element.44.a_ref, f32[16,512]{1,0:T(8,128)S(1)} %get-tuple-element.40.c_ref.refs_0_, ...), custom_call_target="tpu_custom_call" | custom-call | flops 62914560 | bytes 2621440 | tf_op jit(solution)/shard_map/pallas_call | solution.py:55
  37.6 3.0 %all-to-all-start.2 = ((bf16[32,8,80]{2,1,0:T(8,128)(2,1)}), bf16[32,8,80]{2,1,0:T(8,128)(2,1)S(1)}, u32[]{:S(2)}, u32[]{:S(2)}) async-start(bf16[32,8,80]{2,1,0:T(8,128)(2,1)} %get-tuple-element.50), calls=%async_computation.2 | async-start | bytes 131072 | tf_op jit(solution)/shard_map/all_to_all | solution.py:82
  40.6 2.4 %shard_map.101 = (bf16[512,1280]{1,0:T(8,128)(2,1)}, bf16[512,1280]{1,0:T(8,128)(2,1)}, f32[8,128]{1,0:T(8,128)}) custom-call(f32[16,512]{1,0:T(8,128)S(1)} %get-tuple-element.40.c_ref.refs_0_, f32[16,512]{1,0:T(8,128)S(1)} %get-tuple-element.41.d_ref.refs_1_, bf16[16,512]{1,0:T(8,128)(2,1)S(1)} %get-tuple-element.45.refs_2_, ...), custom_call_target="tpu_custom_call" | custom-call | flops 68719476736 | bytes 2621440 | tf_op jit(solution)/shard_map/pallas_call | solution.py:55
  43.1 4.8 %all-to-all-done.2.in_ref = bf16[32,8,80]{2,1,0:T(8,128)(2,1)S(1)} async-done(((bf16[32,8,80]{2,1,0:T(8,128)(2,1)}), bf16[32,8,80]{2,1,0:T(8,128)(2,1)S(1)}, u32[]{:S(2)}, u32[]{:S(2)}) %all-to-all-start.2) | async-done | bytes 40992 | tf_op jit(solution)/shard_map/all_to_all | solution.py:82
  47.9 0.7 %shard_map.102 = f32[16,40]{1,0:T(8,128)} custom-call(bf16[32,8,80]{2,1,0:T(8,128)(2,1)S(1)} %all-to-all-done.2.in_ref), custom_call_target="tpu_custom_call" | custom-call | flops 20480 | bytes 81920 | tf_op jit(solution)/shard_map/pallas_call | solution.py:55
  (1 shorter events, 0.0 us)
Async XLA Ops:
  0.6 1.3 %copy-start = (bf16[1,512,1280]{2,1,0:T(8,128)(2,1)S(1)}, bf16[1,512,1280]{2,1,0:T(8,128)(2,1)}, u32[]{:S(2)}) copy-start(bf16[1,512,1280]{2,1,0:T(8,128)(2,1)} %param.5) | copy-start | bytes 3932164
  0.6 1.3 %copy-start.4 = (bf16[1280,16]{0,1:T(8,128)(2,1)S(1)}, bf16[1280,16]{0,1:T(8,128)(2,1)}, u32[]{:S(2)}) copy-start(bf16[1280,16]{0,1:T(8,128)(2,1)} %param.6) | copy-start | bytes 122884
  0.7 2.1 %copy-start.1 = (bf16[1,512,1280]{2,1,0:T(8,128)(2,1)S(1)}, bf16[1,512,1280]{2,1,0:T(8,128)(2,1)}, u32[]{:S(2)}) copy-start(bf16[1,512,1280]{2,1,0:T(8,128)(2,1)} %param.9) | copy-start | bytes 3932164
  3.0 1.5 %collective-permute-start = (f32[16,2048]{1,0:T(8,128)S(1)}, f32[16,2048]{1,0:T(8,128)S(1)}, u32[]{:S(2)}, u32[]{:S(2)}) collective-permute-start(f32[16,2048]{1,0:T(8,128)S(1)} %get-tuple-element.31.l_ref), channel_id=1, source_target_pairs={{0,8},{8,0},{16,24},{24,16},{1,9},{9,1},{17,25},{25,17},{2,10},{10... | collective-permute-start | bytes 393224 | tf_op jit(solution)/shard_map/ppermute | solution.py:79
  4.5 15.2 %copy-start.2 = (bf16[1,1280,1280]{2,1,0:T(8,128)(2,1)S(1)}, bf16[1,1280,1280]{2,1,0:T(8,128)(2,1)}, u32[]{:S(2)}) copy-start(bf16[1,1280,1280]{2,1,0:T(8,128)(2,1)} %param.8) | copy-start | bytes 9830404
  4.5 15.2 %copy-start.3 = (bf16[1,1280,1280]{2,1,0:T(8,128)(2,1)S(1)}, bf16[1,1280,1280]{2,1,0:T(8,128)(2,1)}, u32[]{:S(2)}) copy-start(bf16[1,1280,1280]{2,1,0:T(8,128)(2,1)} %param.7) | copy-start | bytes 9830404
  22.6 1.8 %collective-permute-start.2 = (f32[16,1280]{1,0:T(8,128)S(1)}, f32[16,1280]{1,0:T(8,128)S(1)}, u32[]{:S(2)}, u32[]{:S(2)}) collective-permute-start(f32[16,1280]{1,0:T(8,128)S(1)} %get-tuple-element.43), channel_id=1, source_target_pairs={{0,8},{8,0},{16,24},{24,16},{1,9},{9,1},{17,25},{25,17},{2,10},{10... | collective-permute-start | bytes 245768 | tf_op jit(solution)/shard_map/ppermute | solution.py:79
  22.8 8.3 %collective-permute-start.1 = (f32[16,1408]{1,0:T(8,128)S(1)}, f32[16,1408]{1,0:T(8,128)S(1)}, u32[]{:S(2)}, u32[]{:S(2)}) collective-permute-start(f32[16,1408]{1,0:T(8,128)S(1)} %get-tuple-element.39.l_ref), channel_id=1, source_target_pairs={{0,16},{8,24},{16,0},{24,8},{1,17},{9,25},{17,1},{25,9},{2,18},{10... | collective-permute-start | bytes 270344 | tf_op jit(solution)/shard_map/ppermute | solution.py:79
  25.0 10.8 %all-to-all-start.1 = ((bf16[32,2,1280]{2,1,0:T(2,128)(2,1)}), bf16[32,2,1280]{2,1,0:T(2,128)(2,1)S(1)}, u32[]{:S(2)}, u32[]{:S(2)}) async-start(bf16[32,2,1280]{2,1,0:T(2,128)(2,1)} %shard_map.99), calls=%async_computation.1 | async-start | bytes 327680 | tf_op jit(solution)/shard_map/all_to_all | solution.py:82
  37.6 10.3 %all-to-all-start.2 = ((bf16[32,8,80]{2,1,0:T(8,128)(2,1)}), bf16[32,8,80]{2,1,0:T(8,128)(2,1)S(1)}, u32[]{:S(2)}, u32[]{:S(2)}) async-start(bf16[32,8,80]{2,1,0:T(8,128)(2,1)} %get-tuple-element.50), calls=%async_computation.2 | async-start | bytes 131072 | tf_op jit(solution)/shard_map/all_to_all | solution.py:82

commit v6 on v3

--- a/solution.py
+++ b/solution.py
@@ -115,23 +115,22 @@
         in_hbm=(2,),
     )(feats, router.T, begun)
 
-    def cotangent_kernel(p_ref, c_ref, g_ref, part_ref, keep_ref, half_ref):
-        part_ref[:, :wide] = p_ref[...]
+    def cotangent_kernel(c_ref, g_ref, out_ref, keep_ref, half_ref):
         b = dot(c_ref[...], g_ref[...], 1, 0)
         half_ref[0] = b[:, :half]
         half_ref[1] = b[:, half:]
         core = lax.rem(lax.axis_index("seq"), 2)
-        part_ref[:, wide:] = half_ref[1 - core]
+        out_ref[...] = half_ref[1 - core]
         keep_ref[...] = half_ref[core]
 
-    part, keep = call(
+    out, keep = call(
         cotangent_kernel,
-        [((slots, wide + half), F32), ((slots, half), F32)],
+        [((slots, half), F32)] * 2,
         24,
         2 * slots * length * width,
         2 * length * width,
         [pltpu.VMEM((2, slots, half), F32)],
-    )(part, combine_b, cotangent)
+    )(combine_b, cotangent)
 
     def merged(l_ref, r_ref):
         tops, totals, totals_b = (
@@ -142,14 +141,14 @@
         total, total_b = (scale[0] * v[0] + scale[1] * v[1] for v in (totals, totals_b))
         return scale[0] * l_ref[:, :width] + scale[1] * r_ref[:, :width], top, total, total_b
 
-    def pack_kernel(l_ref, r_ref, keep_ref, part_ref, send_ref, half_ref):
+    def pack_kernel(l_ref, r_ref, keep_ref, their_ref, part_ref, send_ref, half_ref):
         a, top, total, total_b = merged(l_ref, r_ref)
         part_ref[:, :width] = a
         part_ref[:, width:] = stat_tile(top, total, total_b)
         half_ref[0] = a[:, :half]
         half_ref[1] = a[:, half:]
         a = half_ref[lax.rem(lax.axis_index("seq"), 2)]
-        b = keep_ref[...] + r_ref[:, wide:]
+        b = keep_ref[...] + their_ref[...]
         rows = jnp.concatenate([a, b, stat_tile(*pieces(top), *pieces(total_b))], axis=1)
         for e in range(ne):
             chunk = rows[e * per : (e + 1) * per].astype(BF16)
@@ -163,7 +162,7 @@
         PACK_FLOPS,
         8 * slots * wide,
         [pltpu.VMEM((2, slots, half), F32)],
-    )(part, to_seq(part, 1), keep)
+    )(part, to_seq(part, 1), keep, to_seq(out, 1))
     rows_in = to_all(send)
 
     def expert_kernel(*refs):

time: 48.9 us -> 48.9 us (level)
    ppermute x3 -> x4, waiting for transfers between devices: 0.99 us -> 1.17 us  [to_seq(): return lax.ppermute(x, 'seq', [(i, i ^ k) for i in range(ns)])]
    ppermute x3 -> x4, starting transfers between devices: 2.23 us -> 2.3 us  [to_seq(): return lax.ppermute(x, 'seq', [(i, i ^ k) for i in range(ns)])]
  transfers between devices with their start and end apart: 5 -> 6, of which waited for: 3 -> 3; matrix products, arithmetic and copies ran while one was open for 0% -> 0% of each run, Pallas kernels for 14% -> 15%
where the time goes in v6:
time: 48.9 us; the launch traced here: 48.6 us
  blocking collectives  14.9 us (30%)
  Pallas kernels  13.3 us (27%)
  waiting for transfers between devices  10.2 us (21%)
  starting transfers between devices  8.19 us (17%)
  local copies, waits for them, and re-layouts  1.3 us (3%)
  between operations  0.73 us (1%)
    all_to_all x1, blocking collectives, to_all(): return lax.all_to_all(x, ('seq', 'exp'), 0, 0, tiled=True)  14.9 us
    pallas_call x11, Pallas kernels, run(): pl.pallas_call(body, out_shape=tuple((jax.ShapeDtypeStruct(s, d) for s, d...  13.3 us
    all_to_all x2, waiting for transfers between devices, to_all(): return lax.all_to_all(x, ('seq', 'exp'), 0, 0, tiled=True)  9.03 us
    all_to_all x2, starting transfers between devices, to_all(): return lax.all_to_all(x, ('seq', 'exp'), 0, 0, tiled=True)  5.89 us
    ppermute x4, starting transfers between devices, to_seq(): return lax.ppermute(x, 'seq', [(i, i ^ k) for i in range(ns)])  2.3 us
    unnamed x10, local copies, waits for them, and re-layouts  1.3 us
    ppermute x4, waiting for transfers between devices, to_seq(): return lax.ppermute(x, 'seq', [(i, i ^ k) for i in range(ns)])  1.17 us
  transfers between devices with their start and end apart: 6, of which 3 were waited for; matrix products, arithmetic and copies ran while one was open for 0% of the time, Pallas kernels for 15%

profile of v6, /device:TPU:0, one launch (start us, length us, event | category | flops | bytes accessed | tf_op | source)
XLA Modules:
  0.0 48.6 jit_solution(10812140587085242153)
XLA Ops:
  0.6 0.0 copy-start
  0.6 0.0 copy-start.4
  0.7 0.0 copy-start.1
  0.7 1.3 %copy-done = bf16[1,512,1280]{2,1,0:T(8,128)(2,1)S(1)} copy-done((bf16[1,512,1280]{2,1,0:T(8,128)(2,1)S(1)}, bf16[1,512,1280]{2,1,0:T(8,128)(2,1)}, u32[]{:S(2)}) %copy-start) | copy-done | bytes 1310744
  1.9 0.0 copy-done.4
  2.0 0.8 %shard_map.93 = (f32[16,1408]{1,0:T(8,128)S(1)}, bf16[16,512]{1,0:T(8,128)(2,1)S(1)}) custom-call(bf16[512,1280]{1,0:T(8,128)(2,1)S(1)} %bitcast.10, bf16[16,1280]{1,0:T(8,128)(2,1)S(1)} %bitcast.17, f32[8,128]{1,0:T(8,128)S(1)} %shard_map.92._), custom_call_target="tpu_custom_call" | custom-call | flops 41943040 | bytes 1310720 | tf_op jit(solution)/shard_map/pallas_call | solution.py:55
  2.7 0.5 collective-permute-start
  3.2 0.0 copy-done.1
  3.2 0.3 shard_map.94
  3.5 0.1 collective-permute-start.1
  3.6 1.2 %collective-permute-done.1.their_ref = f32[16,640]{1,0:T(8,128)S(1)} collective-permute-done((f32[16,640]{1,0:T(8,128)S(1)}, f32[16,640]{1,0:T(8,128)S(1)}, u32[]{:S(2)}, u32[]{:S(2)}) %collective-permute-start.1) | collective-permute-done | bytes 40992 | tf_op jit(solution)/shard_map/ppermute | solution.py:79
  4.7 0.0 collective-permute-done.r_ref
  4.7 0.0 copy-start.2
  4.7 0.0 copy-start.3
  4.7 0.2 shard_map.95
  4.9 14.9 %all_to_all.15.refs_1_ = bf16[32,2,1408]{2,1,0:T(2,128)(2,1)S(1)} all-to-all(bf16[32,2,1408]{2,1,0:T(2,128)(2,1)S(1)} %get-tuple-element.33), channel_id=1, replica_groups=mesh['seq'=4,'exp'=8] {'seq','exp'}, dimensions={0} | all-to-all | bytes 360448 | tf_op jit(solution)/shard_map/all_to_all | solution.py:82
  19.8 0.0 copy-done.2
  19.8 0.0 copy-done.3
  19.8 2.8 %shard_map.96 = (bf16[16,1280]{1,0:T(8,128)(2,1)S(1)}, bf16[16,1280]{1,0:T(8,128)(2,1)S(1)}, bf16[16,1280]{1,0:T(8,128)(2,1)S(1)}, bf16[16,1280]{1,0:T(8,128)(2,...) custom-call(bf16[1280,1280]{1,0:T(8,128)(2,1)S(1)} %bitcast.15, bf16[32,2,1408]{2,1,0:T(2,128)(2,1)S(1)} %all_to_all.15.refs_1_, ...), custom_call_target="tpu_custom_call" | custom-call | flops 209715200 | bytes 6553600 | tf_op jit(solution)/shard_map/pallas_call | solution.py:55
  22.6 0.3 collective-permute-start.3
  22.9 1.5 %collective-permute-start.2 = (f32[16,1408]{1,0:T(8,128)S(1)}, f32[16,1408]{1,0:T(8,128)S(1)}, u32[]{:S(2)}, u32[]{:S(2)}) collective-permute-start(f32[16,1408]{1,0:T(8,128)S(1)} %get-tuple-element.39.l_ref), channel_id=1, source_target_pairs={{0,16},{8,24},{16,0},{24,8},{1,17},{9,25},{17,1},{25,9},{2,18},{10... | collective-permute-start | bytes 270344 | tf_op jit(solution)/shard_map/ppermute | solution.py:79
  24.4 0.0 collective-permute-done.3.r_ref
  24.4 0.7 %shard_map.99 = bf16[32,2,1280]{2,1,0:T(2,128)(2,1)} custom-call(f32[16,1280]{1,0:T(8,128)S(1)} %get-tuple-element.42.l_ref, f32[16,1280]{1,0:T(8,128)S(1)} %collective-permute-done.3.r_ref), custom_call_target="tpu_custom_call" | custom-call | flops 40960 | bytes 163840 | tf_op jit(solution)/shard_map/pallas_call | solution.py:55
  25.1 2.9 %all-to-all-start.1 = ((bf16[32,2,1280]{2,1,0:T(2,128)(2,1)}), bf16[32,2,1280]{2,1,0:T(2,128)(2,1)S(1)}, u32[]{:S(2)}, u32[]{:S(2)}) async-start(bf16[32,2,1280]{2,1,0:T(2,128)(2,1)} %shard_map.99), calls=%async_computation.1 | async-start | bytes 327680 | tf_op jit(solution)/shard_map/all_to_all | solution.py:82
  28.0 3.2 %shard_map.97 = (bf16[1280,1280]{1,0:T(8,128)(2,1)}, bf16[1280,1280]{1,0:T(8,128)(2,1)}, f32[8,128]{1,0:T(8,128)S(1)}) custom-call(bf16[16,1280]{1,0:T(8,128)(2,1)S(1)} %get-tuple-element.34.refs_0_, bf16[16,1280]{1,0:T(8,128)(2,1)S(1)} %get-tuple-element.35.refs_1_, bf16[16,1280]{1,0:T(8,128)(2,1)S(1)} %get-tuple-element.36.refs_2_, ...), custom_call_target="tpu_custom_call" | custom-call | flops 68719476736 | bytes 6553600 | tf_op jit(solution)/shard_map/pallas_call | solution.py:55
  31.2 0.0 collective-permute-done.2.r_ref
  31.2 0.5 shard_map.98
  31.7 4.2 %all-to-all-done.1.in_ref = bf16[32,2,1280]{2,1,0:T(2,128)(2,1)S(1)} async-done(((bf16[32,2,1280]{2,1,0:T(2,128)(2,1)}), bf16[32,2,1280]{2,1,0:T(2,128)(2,1)S(1)}, u32[]{:S(2)}, u32[]{:S(2)}) %all-to-all-start.1) | async-done | bytes 163872 | tf_op jit(solution)/shard_map/all_to_all | solution.py:82
  35.9 1.8 %shard_map.100 = (bf16[16,512]{1,0:T(8,128)(2,1)S(1)}, bf16[16,1280]{1,0:T(8,128)(2,1)S(1)}, bf16[16,1280]{1,0:T(8,128)(2,1)S(1)}, bf16[32,8,80]{2,1,0:T(8,128)(2,1)}) custom-call(bf16[32,2,1280]{2,1,0:T(2,128)(2,1)S(1)} %all-to-all-done.1.in_ref, f32[16,1280]{1,0:T(8,128)S(1)} %get-tuple-element.44.a_ref, f32[16,512]{1,0:T(8,128)S(1)} %get-tuple-element.40.c_ref.refs_0_, ...), custom_call_target="tpu_custom_call" | custom-call | flops 62914560 | bytes 2621440 | tf_op jit(solution)/shard_map/pallas_call | solution.py:55
  37.7 3.0 %all-to-all-start.2 = ((bf16[32,8,80]{2,1,0:T(8,128)(2,1)}), bf16[32,8,80]{2,1,0:T(8,128)(2,1)S(1)}, u32[]{:S(2)}, u32[]{:S(2)}) async-start(bf16[32,8,80]{2,1,0:T(8,128)(2,1)} %get-tuple-element.50), calls=%async_computation.2 | async-start | bytes 131072 | tf_op jit(solution)/shard_map/all_to_all | solution.py:82
  40.6 2.4 %shard_map.101 = (bf16[512,1280]{1,0:T(8,128)(2,1)}, bf16[512,1280]{1,0:T(8,128)(2,1)}, f32[8,128]{1,0:T(8,128)}) custom-call(f32[16,512]{1,0:T(8,128)S(1)} %get-tuple-element.40.c_ref.refs_0_, f32[16,512]{1,0:T(8,128)S(1)} %get-tuple-element.41.d_ref.refs_1_, bf16[16,512]{1,0:T(8,128)(2,1)S(1)} %get-tuple-element.45.refs_2_, ...), custom_call_target="tpu_custom_call" | custom-call | flops 68719476736 | bytes 2621440 | tf_op jit(solution)/shard_map/pallas_call | solution.py:55
  43.1 4.8 %all-to-all-done.2.in_ref = bf16[32,8,80]{2,1,0:T(8,128)(2,1)S(1)} async-done(((bf16[32,8,80]{2,1,0:T(8,128)(2,1)}), bf16[32,8,80]{2,1,0:T(8,128)(2,1)S(1)}, u32[]{:S(2)}, u32[]{:S(2)}) %all-to-all-start.2) | async-done | bytes 40992 | tf_op jit(solution)/shard_map/all_to_all | solution.py:82
  47.9 0.7 %shard_map.102 = f32[16,40]{1,0:T(8,128)} custom-call(bf16[32,8,80]{2,1,0:T(8,128)(2,1)S(1)} %all-to-all-done.2.in_ref), custom_call_target="tpu_custom_call" | custom-call | flops 20480 | bytes 81920 | tf_op jit(solution)/shard_map/pallas_call | solution.py:55
  (1 shorter events, 0.0 us)
Async XLA Ops:
  0.6 1.3 %copy-start = (bf16[1,512,1280]{2,1,0:T(8,128)(2,1)S(1)}, bf16[1,512,1280]{2,1,0:T(8,128)(2,1)}, u32[]{:S(2)}) copy-start(bf16[1,512,1280]{2,1,0:T(8,128)(2,1)} %param.5) | copy-start | bytes 3932164
  0.6 1.3 %copy-start.4 = (bf16[1280,16]{0,1:T(8,128)(2,1)S(1)}, bf16[1280,16]{0,1:T(8,128)(2,1)}, u32[]{:S(2)}) copy-start(bf16[1280,16]{0,1:T(8,128)(2,1)} %param.6) | copy-start | bytes 122884
  0.7 2.5 %copy-start.1 = (bf16[1,512,1280]{2,1,0:T(8,128)(2,1)S(1)}, bf16[1,512,1280]{2,1,0:T(8,128)(2,1)}, u32[]{:S(2)}) copy-start(bf16[1,512,1280]{2,1,0:T(8,128)(2,1)} %param.9) | copy-start | bytes 3932164
  2.7 2.0 %collective-permute-start = (f32[16,1408]{1,0:T(8,128)S(1)}, f32[16,1408]{1,0:T(8,128)S(1)}, u32[]{:S(2)}, u32[]{:S(2)}) collective-permute-start(f32[16,1408]{1,0:T(8,128)S(1)} %get-tuple-element.29.l_ref), channel_id=1, source_target_pairs={{0,8},{8,0},{16,24},{24,16},{1,9},{9,1},{17,25},{25,17},{2,10},{10... | collective-permute-start | bytes 270344 | tf_op jit(solution)/shard_map/ppermute | solution.py:79
  3.5 1.2 %collective-permute-start.1 = (f32[16,640]{1,0:T(8,128)S(1)}, f32[16,640]{1,0:T(8,128)S(1)}, u32[]{:S(2)}, u32[]{:S(2)}) collective-permute-start(f32[16,640]{1,0:T(8,128)S(1)} %get-tuple-element.32), channel_id=1, source_target_pairs={{0,8},{8,0},{16,24},{24,16},{1,9},{9,1},{17,25},{25,17},{2,10},{10... | collective-permute-start | bytes 122888 | tf_op jit(solution)/shard_map/ppermute | solution.py:79
  4.7 15.0 %copy-start.2 = (bf16[1,1280,1280]{2,1,0:T(8,128)(2,1)S(1)}, bf16[1,1280,1280]{2,1,0:T(8,128)(2,1)}, u32[]{:S(2)}) copy-start(bf16[1,1280,1280]{2,1,0:T(8,128)(2,1)} %param.8) | copy-start | bytes 9830404
  4.7 15.0 %copy-start.3 = (bf16[1,1280,1280]{2,1,0:T(8,128)(2,1)S(1)}, bf16[1,1280,1280]{2,1,0:T(8,128)(2,1)}, u32[]{:S(2)}) copy-start(bf16[1,1280,1280]{2,1,0:T(8,128)(2,1)} %param.7) | copy-start | bytes 9830404
  22.6 1.8 %collective-permute-start.3 = (f32[16,1280]{1,0:T(8,128)S(1)}, f32[16,1280]{1,0:T(8,128)S(1)}, u32[]{:S(2)}, u32[]{:S(2)}) collective-permute-start(f32[16,1280]{1,0:T(8,128)S(1)} %get-tuple-element.43), channel_id=1, source_target_pairs={{0,8},{8,0},{16,24},{24,16},{1,9},{9,1},{17,25},{25,17},{2,10},{10... | collective-permute-start | bytes 245768 | tf_op jit(solution)/shard_map/ppermute | solution.py:79
  22.9 8.3 %collective-permute-start.2 = (f32[16,1408]{1,0:T(8,128)S(1)}, f32[16,1408]{1,0:T(8,128)S(1)}, u32[]{:S(2)}, u32[]{:S(2)}) collective-permute-start(f32[16,1408]{1,0:T(8,128)S(1)} %get-tuple-element.39.l_ref), channel_id=1, source_target_pairs={{0,16},{8,24},{16,0},{24,8},{1,17},{9,25},{17,1},{25,9},{2,18},{10... | collective-permute-start | bytes 270344 | tf_op jit(solution)/shard_map/ppermute | solution.py:79
  25.1 10.8 %all-to-all-start.1 = ((bf16[32,2,1280]{2,1,0:T(2,128)(2,1)}), bf16[32,2,1280]{2,1,0:T(2,128)(2,1)S(1)}, u32[]{:S(2)}, u32[]{:S(2)}) async-start(bf16[32,2,1280]{2,1,0:T(2,128)(2,1)} %shard_map.99), calls=%async_computation.1 | async-start | bytes 327680 | tf_op jit(solution)/shard_map/all_to_all | solution.py:82
  37.7 10.3 %all-to-all-start.2 = ((bf16[32,8,80]{2,1,0:T(8,128)(2,1)}), bf16[32,8,80]{2,1,0:T(8,128)(2,1)S(1)}, u32[]{:S(2)}, u32[]{:S(2)}) async-start(bf16[32,8,80]{2,1,0:T(8,128)(2,1)} %get-tuple-element.50), calls=%async_computation.2 | async-start | bytes 131072 | tf_op jit(solution)/shard_map/all_to_all | solution.py:82

commit v7 on v3

--- a/solution.py
+++ b/solution.py
@@ -324,13 +324,13 @@
         d_c = combine * (d_combine - jnp.sum(combine * d_combine, axis=0, keepdims=True))
         d_d = dispatch * (dot(dx, x, 1, 1) - inner)
         d_logit = (d_c + d_d).astype(BF16)
-        d_route = dot(d_logit, x, 1, 0)
+        d_route = dot(d_logit, x, 1, 0).astype(BF16)
         l_ref[...] = d_logit
         y_ref[...] = y
         dx_ref[...] = dx
         for k in range(ns * ne):
             piece = d_route[:, k * cut : (k + 1) * cut]
-            out[k] = jnp.concatenate([piece[: slots // 2], piece[slots // 2 :]], axis=1).astype(BF16)
+            out[k] = jnp.concatenate([piece[: slots // 2], piece[slots // 2 :]], axis=1)
 
     d_logit, y, dx, send = call(
         logit_kernel,

time: 48.9 us -> 48.9 us (level)
  no operation moved by 1% of the time
where the time goes in v7:
time: 48.9 us; the launch traced here: 48.6 us
  blocking collectives  15.1 us (31%)
  Pallas kernels  13.4 us (27%)
  waiting for transfers between devices  10 us (20%)
  starting transfers between devices  8.13 us (17%)
  local copies, waits for them, and re-layouts  1.3 us (3%)
  between operations  0.72 us (1%)
    all_to_all x1, blocking collectives, to_all(): return lax.all_to_all(x, ('seq', 'exp'), 0, 0, tiled=True)  15.1 us
    pallas_call x11, Pallas kernels, run(): pl.pallas_call(body, out_shape=tuple((jax.ShapeDtypeStruct(s, d) for s, d...  13.4 us
    all_to_all x2, waiting for transfers between devices, to_all(): return lax.all_to_all(x, ('seq', 'exp'), 0, 0, tiled=True)  9.03 us
    all_to_all x2, starting transfers between devices, to_all(): return lax.all_to_all(x, ('seq', 'exp'), 0, 0, tiled=True)  5.89 us
    ppermute x3, starting transfers between devices, to_seq(): return lax.ppermute(x, 'seq', [(i, i ^ k) for i in range(ns)])  2.23 us
    unnamed x10, local copies, waits for them, and re-layouts  1.3 us
    ppermute x3, waiting for transfers between devices, to_seq(): return lax.ppermute(x, 'seq', [(i, i ^ k) for i in range(ns)])  0.99 us
  transfers between devices with their start and end apart: 5, of which 3 were waited for; matrix products, arithmetic and copies ran while one was open for 0% of the time, Pallas kernels for 14%

profile of v7, /device:TPU:0, one launch (start us, length us, event | category | flops | bytes accessed | tf_op | source)
XLA Modules:
  0.0 48.6 jit_solution(2331869301134881261)
XLA Ops:
  0.6 0.0 copy-start
  0.6 0.0 copy-start.4
  0.7 0.0 copy-start.1
  0.7 1.3 %copy-done = bf16[1,512,1280]{2,1,0:T(8,128)(2,1)S(1)} copy-done((bf16[1,512,1280]{2,1,0:T(8,128)(2,1)S(1)}, bf16[1,512,1280]{2,1,0:T(8,128)(2,1)}, u32[]{:S(2)}) %copy-start) | copy-done | bytes 1310744
  1.9 0.0 copy-done.4
  2.0 0.8 %shard_map.93 = (f32[16,1408]{1,0:T(8,128)S(1)}, bf16[16,512]{1,0:T(8,128)(2,1)S(1)}) custom-call(bf16[512,1280]{1,0:T(8,128)(2,1)S(1)} %bitcast.10, bf16[16,1280]{1,0:T(8,128)(2,1)S(1)} %bitcast.17, f32[8,128]{1,0:T(8,128)S(1)} %shard_map.92._), custom_call_target="tpu_custom_call" | custom-call | flops 41943040 | bytes 1310720 | tf_op jit(solution)/shard_map/pallas_call | solution.py:55
  2.7 0.0 copy-done.1
  2.7 0.3 shard_map.94
  3.0 0.5 collective-permute-start
  3.5 1.0 %collective-permute-done.r_ref = f32[16,2048]{1,0:T(8,128)S(1)} collective-permute-done((f32[16,2048]{1,0:T(8,128)S(1)}, f32[16,2048]{1,0:T(8,128)S(1)}, u32[]{:S(2)}, u32[]{:S(2)}) %collective-permute-start) | collective-permute-done | bytes 131104 | tf_op jit(solution)/shard_map/ppermute | solution.py:79
  4.5 0.0 copy-start.2
  4.5 0.0 copy-start.3
  4.5 0.2 shard_map.95
  4.7 15.1 %all_to_all.15.refs_1_ = bf16[32,2,1408]{2,1,0:T(2,128)(2,1)S(1)} all-to-all(bf16[32,2,1408]{2,1,0:T(2,128)(2,1)S(1)} %get-tuple-element.33), channel_id=1, replica_groups=mesh['seq'=4,'exp'=8] {'seq','exp'}, dimensions={0} | all-to-all | bytes 360448 | tf_op jit(solution)/shard_map/all_to_all | solution.py:82
  19.7 0.0 copy-done.2
  19.7 0.0 copy-done.3
  19.7 2.8 %shard_map.96 = (bf16[16,1280]{1,0:T(8,128)(2,1)S(1)}, bf16[16,1280]{1,0:T(8,128)(2,1)S(1)}, bf16[16,1280]{1,0:T(8,128)(2,1)S(1)}, bf16[16,1280]{1,0:T(8,128)(2,...) custom-call(bf16[1280,1280]{1,0:T(8,128)(2,1)S(1)} %bitcast.15, bf16[32,2,1408]{2,1,0:T(2,128)(2,1)S(1)} %all_to_all.15.refs_1_, ...), custom_call_target="tpu_custom_call" | custom-call | flops 209715200 | bytes 6553600 | tf_op jit(solution)/shard_map/pallas_call | solution.py:55
  22.6 0.3 collective-permute-start.2
  22.8 1.5 %collective-permute-start.1 = (f32[16,1408]{1,0:T(8,128)S(1)}, f32[16,1408]{1,0:T(8,128)S(1)}, u32[]{:S(2)}, u32[]{:S(2)}) collective-permute-start(f32[16,1408]{1,0:T(8,128)S(1)} %get-tuple-element.39.l_ref), channel_id=1, source_target_pairs={{0,16},{8,24},{16,0},{24,8},{1,17},{9,25},{17,1},{25,9},{2,18},{10... | collective-permute-start | bytes 270344 | tf_op jit(solution)/shard_map/ppermute | solution.py:79
  24.3 0.0 collective-permute-done.2.r_ref
  24.3 0.7 %shard_map.99 = bf16[32,2,1280]{2,1,0:T(2,128)(2,1)} custom-call(f32[16,1280]{1,0:T(8,128)S(1)} %get-tuple-element.42.l_ref, f32[16,1280]{1,0:T(8,128)S(1)} %collective-permute-done.2.r_ref), custom_call_target="tpu_custom_call" | custom-call | flops 40960 | bytes 163840 | tf_op jit(solution)/shard_map/pallas_call | solution.py:55
  25.0 2.9 %all-to-all-start.1 = ((bf16[32,2,1280]{2,1,0:T(2,128)(2,1)}), bf16[32,2,1280]{2,1,0:T(2,128)(2,1)S(1)}, u32[]{:S(2)}, u32[]{:S(2)}) async-start(bf16[32,2,1280]{2,1,0:T(2,128)(2,1)} %shard_map.99), calls=%async_computation.1 | async-start | bytes 327680 | tf_op jit(solution)/shard_map/all_to_all | solution.py:82
  28.0 3.2 %shard_map.97 = (bf16[1280,1280]{1,0:T(8,128)(2,1)}, bf16[1280,1280]{1,0:T(8,128)(2,1)}, f32[8,128]{1,0:T(8,128)S(1)}) custom-call(bf16[16,1280]{1,0:T(8,128)(2,1)S(1)} %get-tuple-element.34.refs_0_, bf16[16,1280]{1,0:T(8,128)(2,1)S(1)} %get-tuple-element.35.refs_1_, bf16[16,1280]{1,0:T(8,128)(2,1)S(1)} %get-tuple-element.36.refs_2_, ...), custom_call_target="tpu_custom_call" | custom-call | flops 68719476736 | bytes 6553600 | tf_op jit(solution)/shard_map/pallas_call | solution.py:55
  31.2 0.0 collective-permute-done.1.r_ref
  31.2 0.5 shard_map.98
  31.7 4.2 %all-to-all-done.1.in_ref = bf16[32,2,1280]{2,1,0:T(2,128)(2,1)S(1)} async-done(((bf16[32,2,1280]{2,1,0:T(2,128)(2,1)}), bf16[32,2,1280]{2,1,0:T(2,128)(2,1)S(1)}, u32[]{:S(2)}, u32[]{:S(2)}) %all-to-all-start.1) | async-done | bytes 163872 | tf_op jit(solution)/shard_map/all_to_all | solution.py:82
  35.9 1.8 %shard_map.100 = (bf16[16,512]{1,0:T(8,128)(2,1)S(1)}, bf16[16,1280]{1,0:T(8,128)(2,1)S(1)}, bf16[16,1280]{1,0:T(8,128)(2,1)S(1)}, bf16[32,8,80]{2,1,0:T(8,128)(2,1)}) custom-call(bf16[32,2,1280]{2,1,0:T(2,128)(2,1)S(1)} %all-to-all-done.1.in_ref, f32[16,1280]{1,0:T(8,128)S(1)} %get-tuple-element.44.a_ref, f32[16,512]{1,0:T(8,128)S(1)} %get-tuple-element.40.c_ref.refs_0_, ...), custom_call_target="tpu_custom_call" | custom-call | flops 62914560 | bytes 2621440 | tf_op jit(solution)/shard_map/pallas_call | solution.py:55
  37.6 3.0 %all-to-all-start.2 = ((bf16[32,8,80]{2,1,0:T(8,128)(2,1)}), bf16[32,8,80]{2,1,0:T(8,128)(2,1)S(1)}, u32[]{:S(2)}, u32[]{:S(2)}) async-start(bf16[32,8,80]{2,1,0:T(8,128)(2,1)} %get-tuple-element.50), calls=%async_computation.2 | async-start | bytes 131072 | tf_op jit(solution)/shard_map/all_to_all | solution.py:82
  40.6 2.4 %shard_map.101 = (bf16[512,1280]{1,0:T(8,128)(2,1)}, bf16[512,1280]{1,0:T(8,128)(2,1)}, f32[8,128]{1,0:T(8,128)}) custom-call(f32[16,512]{1,0:T(8,128)S(1)} %get-tuple-element.40.c_ref.refs_0_, f32[16,512]{1,0:T(8,128)S(1)} %get-tuple-element.41.d_ref.refs_1_, bf16[16,512]{1,0:T(8,128)(2,1)S(1)} %get-tuple-element.45.refs_2_, ...), custom_call_target="tpu_custom_call" | custom-call | flops 68719476736 | bytes 2621440 | tf_op jit(solution)/shard_map/pallas_call | solution.py:55
  43.1 4.8 %all-to-all-done.2.in_ref = bf16[32,8,80]{2,1,0:T(8,128)(2,1)S(1)} async-done(((bf16[32,8,80]{2,1,0:T(8,128)(2,1)}), bf16[32,8,80]{2,1,0:T(8,128)(2,1)S(1)}, u32[]{:S(2)}, u32[]{:S(2)}) %all-to-all-start.2) | async-done | bytes 40992 | tf_op jit(solution)/shard_map/all_to_all | solution.py:82
  47.9 0.7 %shard_map.102 = f32[16,40]{1,0:T(8,128)} custom-call(bf16[32,8,80]{2,1,0:T(8,128)(2,1)S(1)} %all-to-all-done.2.in_ref), custom_call_target="tpu_custom_call" | custom-call | flops 20480 | bytes 81920 | tf_op jit(solution)/shard_map/pallas_call | solution.py:55
  (1 shorter events, 0.0 us)
Async XLA Ops:
  0.6 1.3 %copy-start = (bf16[1,512,1280]{2,1,0:T(8,128)(2,1)S(1)}, bf16[1,512,1280]{2,1,0:T(8,128)(2,1)}, u32[]{:S(2)}) copy-start(bf16[1,512,1280]{2,1,0:T(8,128)(2,1)} %param.5) | copy-start | bytes 3932164
  0.6 1.3 %copy-start.4 = (bf16[1280,16]{0,1:T(8,128)(2,1)S(1)}, bf16[1280,16]{0,1:T(8,128)(2,1)}, u32[]{:S(2)}) copy-start(bf16[1280,16]{0,1:T(8,128)(2,1)} %param.6) | copy-start | bytes 122884
  0.7 2.1 %copy-start.1 = (bf16[1,512,1280]{2,1,0:T(8,128)(2,1)S(1)}, bf16[1,512,1280]{2,1,0:T(8,128)(2,1)}, u32[]{:S(2)}) copy-start(bf16[1,512,1280]{2,1,0:T(8,128)(2,1)} %param.9) | copy-start | bytes 3932164
  3.0 1.5 %collective-permute-start = (f32[16,2048]{1,0:T(8,128)S(1)}, f32[16,2048]{1,0:T(8,128)S(1)}, u32[]{:S(2)}, u32[]{:S(2)}) collective-permute-start(f32[16,2048]{1,0:T(8,128)S(1)} %get-tuple-element.31.l_ref), channel_id=1, source_target_pairs={{0,8},{8,0},{16,24},{24,16},{1,9},{9,1},{17,25},{25,17},{2,10},{10... | collective-permute-start | bytes 393224 | tf_op jit(solution)/shard_map/ppermute | solution.py:79
  4.5 15.2 %copy-start.2 = (bf16[1,1280,1280]{2,1,0:T(8,128)(2,1)S(1)}, bf16[1,1280,1280]{2,1,0:T(8,128)(2,1)}, u32[]{:S(2)}) copy-start(bf16[1,1280,1280]{2,1,0:T(8,128)(2,1)} %param.8) | copy-start | bytes 9830404
  4.5 15.2 %copy-start.3 = (bf16[1,1280,1280]{2,1,0:T(8,128)(2,1)S(1)}, bf16[1,1280,1280]{2,1,0:T(8,128)(2,1)}, u32[]{:S(2)}) copy-start(bf16[1,1280,1280]{2,1,0:T(8,128)(2,1)} %param.7) | copy-start | bytes 9830404
  22.6 1.8 %collective-permute-start.2 = (f32[16,1280]{1,0:T(8,128)S(1)}, f32[16,1280]{1,0:T(8,128)S(1)}, u32[]{:S(2)}, u32[]{:S(2)}) collective-permute-start(f32[16,1280]{1,0:T(8,128)S(1)} %get-tuple-element.43), channel_id=1, source_target_pairs={{0,8},{8,0},{16,24},{24,16},{1,9},{9,1},{17,25},{25,17},{2,10},{10... | collective-permute-start | bytes 245768 | tf_op jit(solution)/shard_map/ppermute | solution.py:79
  22.8 8.3 %collective-permute-start.1 = (f32[16,1408]{1,0:T(8,128)S(1)}, f32[16,1408]{1,0:T(8,128)S(1)}, u32[]{:S(2)}, u32[]{:S(2)}) collective-permute-start(f32[16,1408]{1,0:T(8,128)S(1)} %get-tuple-element.39.l_ref), channel_id=1, source_target_pairs={{0,16},{8,24},{16,0},{24,8},{1,17},{9,25},{17,1},{25,9},{2,18},{10... | collective-permute-start | bytes 270344 | tf_op jit(solution)/shard_map/ppermute | solution.py:79
  25.0 10.8 %all-to-all-start.1 = ((bf16[32,2,1280]{2,1,0:T(2,128)(2,1)}), bf16[32,2,1280]{2,1,0:T(2,128)(2,1)S(1)}, u32[]{:S(2)}, u32[]{:S(2)}) async-start(bf16[32,2,1280]{2,1,0:T(2,128)(2,1)} %shard_map.99), calls=%async_computation.1 | async-start | bytes 327680 | tf_op jit(solution)/shard_map/all_to_all | solution.py:82
  37.6 10.3 %all-to-all-start.2 = ((bf16[32,8,80]{2,1,0:T(8,128)(2,1)}), bf16[32,8,80]{2,1,0:T(8,128)(2,1)S(1)}, u32[]{:S(2)}, u32[]{:S(2)}) async-start(bf16[32,8,80]{2,1,0:T(8,128)(2,1)} %get-tuple-element.50), calls=%async_computation.2 | async-start | bytes 131072 | tf_op jit(solution)/shard_map/all_to_all | solution.py:82

commit v8 on v3

--- a/solution.py
+++ b/solution.py
@@ -210,14 +210,14 @@
             half_ref[core, :, :half] = y[:, at]
             half_ref[core, :, half:] = dx[:, at]
         core = lax.rem(lax.axis_index("seq"), 2)
-        out_ref[...] = half_ref[1 - core]
+        out_ref[...] = half_ref[1 - core].astype(BF16)
         keep_ref[...] = half_ref[core]
 
     x_rows, dy_rows, act, dh, out, keep = call(
         expert_kernel,
         [((slots, width), BF16)] * 2
         + [((slots, hidden_part), BF16)] * 2
-        + [((slots, width), F32)] * 2,
+        + [((slots, width), BF16), ((slots, width), F32)],
         EXPERT_MIB,
         8 * slots * width * hidden_part,
         4 * width * hidden_part,
@@ -227,7 +227,7 @@
     )(w2, rows_in, w1)
 
     def pack_back_kernel(l_ref, r_ref, send_ref):
-        full = l_ref[...] + r_ref[...]
+        full = l_ref[...] + r_ref[...].astype(F32)
         for c in range(ne):
             chunk = full[c * per : (c + 1) * per].astype(BF16)
             for s in range(ns):

time: 48.9 us -> 48.9 us (level)
  no operation moved by 1% of the time
where the time goes in v8:
time: 48.9 us; the launch traced here: 48.6 us
  blocking collectives  15.1 us (31%)
  Pallas kernels  13.4 us (27%)
  waiting for transfers between devices  10 us (20%)
  starting transfers between devices  8.14 us (17%)
  local copies, waits for them, and re-layouts  1.3 us (3%)
  between operations  0.72 us (1%)
    all_to_all x1, blocking collectives, to_all(): return lax.all_to_all(x, ('seq', 'exp'), 0, 0, tiled=True)  15.1 us
    pallas_call x11, Pallas kernels, run(): pl.pallas_call(body, out_shape=tuple((jax.ShapeDtypeStruct(s, d) for s, d...  13.4 us
    all_to_all x2, waiting for transfers between devices, to_all(): return lax.all_to_all(x, ('seq', 'exp'), 0, 0, tiled=True)  9.04 us
    all_to_all x2, starting transfers between devices, to_all(): return lax.all_to_all(x, ('seq', 'exp'), 0, 0, tiled=True)  5.9 us
    ppermute x3, starting transfers between devices, to_seq(): return lax.ppermute(x, 'seq', [(i, i ^ k) for i in range(ns)])  2.24 us
    unnamed x10, local copies, waits for them, and re-layouts  1.3 us
    ppermute x3, waiting for transfers between devices, to_seq(): return lax.ppermute(x, 'seq', [(i, i ^ k) for i in range(ns)])  0.99 us
  transfers between devices with their start and end apart: 5, of which 3 were waited for; matrix products, arithmetic and copies ran while one was open for 0% of the time, Pallas kernels for 14%

profile of v8, /device:TPU:0, one launch (start us, length us, event | category | flops | bytes accessed | tf_op | source)
XLA Modules:
  0.0 48.6 jit_solution(9414833433463026349)
XLA Ops:
  0.6 0.0 copy-start
  0.6 0.0 copy-start.4
  0.7 0.0 copy-start.1
  0.7 1.3 %copy-done = bf16[1,512,1280]{2,1,0:T(8,128)(2,1)S(1)} copy-done((bf16[1,512,1280]{2,1,0:T(8,128)(2,1)S(1)}, bf16[1,512,1280]{2,1,0:T(8,128)(2,1)}, u32[]{:S(2)}) %copy-start) | copy-done | bytes 1310744
  1.9 0.0 copy-done.4
  2.0 0.8 %shard_map.93 = (f32[16,1408]{1,0:T(8,128)S(1)}, bf16[16,512]{1,0:T(8,128)(2,1)S(1)}) custom-call(bf16[512,1280]{1,0:T(8,128)(2,1)S(1)} %bitcast.10, bf16[16,1280]{1,0:T(8,128)(2,1)S(1)} %bitcast.17, f32[8,128]{1,0:T(8,128)S(1)} %shard_map.92._), custom_call_target="tpu_custom_call" | custom-call | flops 41943040 | bytes 1310720 | tf_op jit(solution)/shard_map/pallas_call | solution.py:55
  2.7 0.0 copy-done.1
  2.7 0.3 shard_map.94
  3.0 0.5 collective-permute-start
  3.5 1.0 %collective-permute-done.r_ref = f32[16,2048]{1,0:T(8,128)S(1)} collective-permute-done((f32[16,2048]{1,0:T(8,128)S(1)}, f32[16,2048]{1,0:T(8,128)S(1)}, u32[]{:S(2)}, u32[]{:S(2)}) %collective-permute-start) | collective-permute-done | bytes 131104 | tf_op jit(solution)/shard_map/ppermute | solution.py:79
  4.5 0.0 copy-start.2
  4.5 0.0 copy-start.3
  4.5 0.2 shard_map.95
  4.7 15.1 %all_to_all.15.refs_1_ = bf16[32,2,1408]{2,1,0:T(2,128)(2,1)S(1)} all-to-all(bf16[32,2,1408]{2,1,0:T(2,128)(2,1)S(1)} %get-tuple-element.33), channel_id=1, replica_groups=mesh['seq'=4,'exp'=8] {'seq','exp'}, dimensions={0} | all-to-all | bytes 360448 | tf_op jit(solution)/shard_map/all_to_all | solution.py:82
  19.7 0.0 copy-done.2
  19.7 0.0 copy-done.3
  19.7 2.8 %shard_map.96 = (bf16[16,1280]{1,0:T(8,128)(2,1)S(1)}, bf16[16,1280]{1,0:T(8,128)(2,1)S(1)}, bf16[16,1280]{1,0:T(8,128)(2,1)S(1)}, bf16[16,1280]{1,0:T(8,128)(2,...) custom-call(bf16[1280,1280]{1,0:T(8,128)(2,1)S(1)} %bitcast.15, ...), custom_call_target="tpu_custom_call" | custom-call | flops 209715200 | bytes 6553600 | tf_op jit(solution)/shard_map/pallas_call | solution.py:55
  22.6 0.3 collective-permute-start.2
  22.9 1.5 %collective-permute-start.1 = (f32[16,1408]{1,0:T(8,128)S(1)}, f32[16,1408]{1,0:T(8,128)S(1)}, u32[]{:S(2)}, u32[]{:S(2)}) collective-permute-start(f32[16,1408]{1,0:T(8,128)S(1)} %get-tuple-element.39.l_ref), channel_id=1, source_target_pairs={{0,16},{8,24},{16,0},{24,8},{1,17},{9,25},{17,1},{25,9},{2,18},{10... | collective-permute-start | bytes 270344 | tf_op jit(solution)/shard_map/ppermute | solution.py:79
  24.3 0.0 collective-permute-done.2.r_ref
  24.3 0.7 %shard_map.99 = bf16[32,2,1280]{2,1,0:T(2,128)(2,1)} custom-call(f32[16,1280]{1,0:T(8,128)S(1)} %get-tuple-element.42.l_ref, bf16[16,1280]{1,0:T(8,128)(2,1)S(1)} %collective-permute-done.2.r_ref), custom_call_target="tpu_custom_call" | custom-call | flops 40960 | bytes 163840 | tf_op jit(solution)/shard_map/pallas_call | solution.py:55
  25.0 2.9 %all-to-all-start.1 = ((bf16[32,2,1280]{2,1,0:T(2,128)(2,1)}), bf16[32,2,1280]{2,1,0:T(2,128)(2,1)S(1)}, u32[]{:S(2)}, u32[]{:S(2)}) async-start(bf16[32,2,1280]{2,1,0:T(2,128)(2,1)} %shard_map.99), calls=%async_computation.1 | async-start | bytes 327680 | tf_op jit(solution)/shard_map/all_to_all | solution.py:82
  28.0 3.2 %shard_map.97 = (bf16[1280,1280]{1,0:T(8,128)(2,1)}, bf16[1280,1280]{1,0:T(8,128)(2,1)}, f32[8,128]{1,0:T(8,128)S(1)}) custom-call(bf16[16,1280]{1,0:T(8,128)(2,1)S(1)} %get-tuple-element.34.refs_0_, bf16[16,1280]{1,0:T(8,128)(2,1)S(1)} %get-tuple-element.35.refs_1_, bf16[16,1280]{1,0:T(8,128)(2,1)S(1)} %get-tuple-element.36.refs_2_, ...), custom_call_target="tpu_custom_call" | custom-call | flops 68719476736 | bytes 6553600 | tf_op jit(solution)/shard_map/pallas_call | solution.py:55
  31.2 0.0 collective-permute-done.1.r_ref
  31.2 0.5 shard_map.98
  31.7 4.2 %all-to-all-done.1.in_ref = bf16[32,2,1280]{2,1,0:T(2,128)(2,1)S(1)} async-done(((bf16[32,2,1280]{2,1,0:T(2,128)(2,1)}), bf16[32,2,1280]{2,1,0:T(2,128)(2,1)S(1)}, u32[]{:S(2)}, u32[]{:S(2)}) %all-to-all-start.1) | async-done | bytes 163872 | tf_op jit(solution)/shard_map/all_to_all | solution.py:82
  35.9 1.8 %shard_map.100 = (bf16[16,512]{1,0:T(8,128)(2,1)S(1)}, bf16[16,1280]{1,0:T(8,128)(2,1)S(1)}, bf16[16,1280]{1,0:T(8,128)(2,1)S(1)}, bf16[32,8,80]{2,1,0:T(8,128)(2,1)}) custom-call(bf16[32,2,1280]{2,1,0:T(2,128)(2,1)S(1)} %all-to-all-done.1.in_ref, f32[16,1280]{1,0:T(8,128)S(1)} %get-tuple-element.44.a_ref, f32[16,512]{1,0:T(8,128)S(1)} %get-tuple-element.40.c_ref.refs_0_, ...), custom_call_target="tpu_custom_call" | custom-call | flops 62914560 | bytes 2621440 | tf_op jit(solution)/shard_map/pallas_call | solution.py:55
  37.6 3.0 %all-to-all-start.2 = ((bf16[32,8,80]{2,1,0:T(8,128)(2,1)}), bf16[32,8,80]{2,1,0:T(8,128)(2,1)S(1)}, u32[]{:S(2)}, u32[]{:S(2)}) async-start(bf16[32,8,80]{2,1,0:T(8,128)(2,1)} %get-tuple-element.50), calls=%async_computation.2 | async-start | bytes 131072 | tf_op jit(solution)/shard_map/all_to_all | solution.py:82
  40.6 2.4 %shard_map.101 = (bf16[512,1280]{1,0:T(8,128)(2,1)}, bf16[512,1280]{1,0:T(8,128)(2,1)}, f32[8,128]{1,0:T(8,128)}) custom-call(f32[16,512]{1,0:T(8,128)S(1)} %get-tuple-element.40.c_ref.refs_0_, f32[16,512]{1,0:T(8,128)S(1)} %get-tuple-element.41.d_ref.refs_1_, bf16[16,512]{1,0:T(8,128)(2,1)S(1)} %get-tuple-element.45.refs_2_, ...), custom_call_target="tpu_custom_call" | custom-call | flops 68719476736 | bytes 2621440 | tf_op jit(solution)/shard_map/pallas_call | solution.py:55
  43.1 4.8 %all-to-all-done.2.in_ref = bf16[32,8,80]{2,1,0:T(8,128)(2,1)S(1)} async-done(((bf16[32,8,80]{2,1,0:T(8,128)(2,1)}), bf16[32,8,80]{2,1,0:T(8,128)(2,1)S(1)}, u32[]{:S(2)}, u32[]{:S(2)}) %all-to-all-start.2) | async-done | bytes 40992 | tf_op jit(solution)/shard_map/all_to_all | solution.py:82
  47.9 0.7 %shard_map.102 = f32[16,40]{1,0:T(8,128)} custom-call(bf16[32,8,80]{2,1,0:T(8,128)(2,1)S(1)} %all-to-all-done.2.in_ref), custom_call_target="tpu_custom_call" | custom-call | flops 20480 | bytes 81920 | tf_op jit(solution)/shard_map/pallas_call | solution.py:55
  (1 shorter events, 0.0 us)
Async XLA Ops:
  0.6 1.3 %copy-start = (bf16[1,512,1280]{2,1,0:T(8,128)(2,1)S(1)}, bf16[1,512,1280]{2,1,0:T(8,128)(2,1)}, u32[]{:S(2)}) copy-start(bf16[1,512,1280]{2,1,0:T(8,128)(2,1)} %param.5) | copy-start | bytes 3932164
  0.6 1.3 %copy-start.4 = (bf16[1280,16]{0,1:T(8,128)(2,1)S(1)}, bf16[1280,16]{0,1:T(8,128)(2,1)}, u32[]{:S(2)}) copy-start(bf16[1280,16]{0,1:T(8,128)(2,1)} %param.6) | copy-start | bytes 122884
  0.7 2.1 %copy-start.1 = (bf16[1,512,1280]{2,1,0:T(8,128)(2,1)S(1)}, bf16[1,512,1280]{2,1,0:T(8,128)(2,1)}, u32[]{:S(2)}) copy-start(bf16[1,512,1280]{2,1,0:T(8,128)(2,1)} %param.9) | copy-start | bytes 3932164
  3.0 1.5 %collective-permute-start = (f32[16,2048]{1,0:T(8,128)S(1)}, f32[16,2048]{1,0:T(8,128)S(1)}, u32[]{:S(2)}, u32[]{:S(2)}) collective-permute-start(f32[16,2048]{1,0:T(8,128)S(1)} %get-tuple-element.31.l_ref), channel_id=1, source_target_pairs={{0,8},{8,0},{16,24},{24,16},{1,9},{9,1},{17,25},{25,17},{2,10},{10... | collective-permute-start | bytes 393224 | tf_op jit(solution)/shard_map/ppermute | solution.py:79
  4.5 15.2 %copy-start.2 = (bf16[1,1280,1280]{2,1,0:T(8,128)(2,1)S(1)}, bf16[1,1280,1280]{2,1,0:T(8,128)(2,1)}, u32[]{:S(2)}) copy-start(bf16[1,1280,1280]{2,1,0:T(8,128)(2,1)} %param.8) | copy-start | bytes 9830404
  4.5 15.2 %copy-start.3 = (bf16[1,1280,1280]{2,1,0:T(8,128)(2,1)S(1)}, bf16[1,1280,1280]{2,1,0:T(8,128)(2,1)}, u32[]{:S(2)}) copy-start(bf16[1,1280,1280]{2,1,0:T(8,128)(2,1)} %param.7) | copy-start | bytes 9830404
  22.6 1.8 %collective-permute-start.2 = (bf16[16,1280]{1,0:T(8,128)(2,1)S(1)}, bf16[16,1280]{1,0:T(8,128)(2,1)S(1)}, u32[]{:S(2)}, u32[]{:S(2)}) collective-permute-start(bf16[16,1280]{1,0:T(8,128)(2,1)S(1)} %get-tuple-element.43), channel_id=1, source_target_pairs={{0,8},{8,0},{16,24},{24,16},{1,9},{9,1},{17,25},{25,17},{2,10},{10... | collective-permute-start | bytes 122888 | tf_op jit(solution)/shard_map/ppermute | solution.py:79
  22.9 8.3 %collective-permute-start.1 = (f32[16,1408]{1,0:T(8,128)S(1)}, f32[16,1408]{1,0:T(8,128)S(1)}, u32[]{:S(2)}, u32[]{:S(2)}) collective-permute-start(f32[16,1408]{1,0:T(8,128)S(1)} %get-tuple-element.39.l_ref), channel_id=1, source_target_pairs={{0,16},{8,24},{16,0},{24,8},{1,17},{9,25},{17,1},{25,9},{2,18},{10... | collective-permute-start | bytes 270344 | tf_op jit(solution)/shard_map/ppermute | solution.py:79
  25.0 10.8 %all-to-all-start.1 = ((bf16[32,2,1280]{2,1,0:T(2,128)(2,1)}), bf16[32,2,1280]{2,1,0:T(2,128)(2,1)S(1)}, u32[]{:S(2)}, u32[]{:S(2)}) async-start(bf16[32,2,1280]{2,1,0:T(2,128)(2,1)} %shard_map.99), calls=%async_computation.1 | async-start | bytes 327680 | tf_op jit(solution)/shard_map/all_to_all | solution.py:82
  37.6 10.3 %all-to-all-start.2 = ((bf16[32,8,80]{2,1,0:T(8,128)(2,1)}), bf16[32,8,80]{2,1,0:T(8,128)(2,1)S(1)}, u32[]{:S(2)}, u32[]{:S(2)}) async-start(bf16[32,8,80]{2,1,0:T(8,128)(2,1)} %get-tuple-element.50), calls=%async_computation.2 | async-start | bytes 131072 | tf_op jit(solution)/shard_map/all_to_all | solution.py:82
